TPU v7x, 256 devices: a whole 4x4x8 slice. The times are simulated.
256 devices in a mesh: wide: 16 (over x, z_hi, core), narrow: 16 (over z_lo, y).
Axes of the slice: x: 4, y: 4, z: 8 (z_hi: 2, z_lo: 4; z = z_hi * 4 + z_lo), core: 2. Of those that a mesh axis runs over, the one named last changes fastest.
Arguments:
- inputs: bfloat16 [131072, 1024], P(('wide', 'narrow')), may hold values from -24 to 24
- w_first: bfloat16 [1024, 1024], replicated, may hold values from -0.1875 to 0.1875
- w_second: bfloat16 [1024, 256], replicated, may hold values from -0.1875 to 0.1875
- requests: int32 [4096, 128], P(('wide', 'narrow')), may hold values from 0 to 511
- slots: int32 [131072, 15], P(('wide', 'narrow')), may hold values from 0 to 2047
- counts: int32 [131072], P(('wide', 'narrow')), may hold values from 1 to 15
- edge_weight: int32 [131072, 15], P(('wide', 'narrow')), may hold values from 1 to 4
- offsets: int32 [4], replicated, may hold values from 0 to 511
Outputs:
- grad_first: float32 [1024, 1024], P('wide')
- grad_second: float32 [1024, 256], P('wide')
Inputs may be any that keep to these rules, and one draw needn't show every extreme that they name: requests of block d only name rows of blocks with the same narrow index as d.
All inputs are finite; a program needn't handle non-finite values.
Results may differ from a plain program's by a relative error of at most 0.0018.
Values may be sent and summed in bfloat16 or wider, within the bound.
A program may use at most 64 MiB of HBM per device.

v0:
```python
import math

import jax
import jax.numpy as jnp
from jax import lax
from jax.sharding import PartitionSpec as P

NEGW = 8


def from_behind(block, axis, distance):
    devices = range(lax.axis_size(axis))
    route = [((i - distance) % len(devices), i) for i in devices]
    return lax.ppermute(block, axis, route)


def sent_together(arrays, axis, dim, along):
    ends, at = ([], 0)
    for a in arrays[:-1]:
        at += a.shape[along]
        ends.append(at)
    both = jnp.concatenate(arrays, axis=along)
    return tuple(
        jnp.split(lax.psum_scatter(both, axis, scatter_dimension=dim, tiled=True), ends, axis=along)
    )


def sent_to_all(value, axis):
    copies = jnp.broadcast_to(value, (lax.axis_size(axis), *value.shape))
    return lax.all_to_all(copies, axis, split_axis=0, concat_axis=0, tiled=True)


def over_copies(value, axis):
    return sent_to_all(value, axis).sum(axis=0)


def in_one(arrays, axis):
    ravelled, at, outs = (jnp.concatenate([a.reshape(-1) for a in arrays]), 0, [])
    so_far = over_copies(ravelled, axis)
    for a in arrays:
        outs.append(so_far[at : at + a.size].reshape(a.shape))
        at += a.size
    return tuple(outs)


def forward(block, w_first, w_second):
    pre = jnp.dot(block, w_first, preferred_element_type=jnp.float32)
    hidden = jnp.maximum(pre, 0.0).astype(jnp.bfloat16)
    codes = jnp.dot(hidden, w_second, preferred_element_type=jnp.float32)
    return (pre, hidden, codes)


def attract(codes, near, weight):
    diff = codes[:, None, :] - near.astype(jnp.float32)
    dist = jnp.sum(diff * diff, axis=-1) / diff.shape[-1]
    return jnp.sum((weight / (1.0 + dist))[:, :, None] * diff, axis=1)


def repel(codes, far):
    diff = codes[:, None, :] - far.astype(jnp.float32)
    dist = jnp.sum(diff * diff, axis=-1) / diff.shape[-1]
    onep = 1.0 + dist
    coef = 1.0 / (onep * onep * (dist / onep + 0.1))
    return -jnp.sum(coef[:, :, None] * diff, axis=1)


def negatives(block, offset, count):
    rows = block.shape[0]
    index = (
        jnp.arange(rows, dtype=jnp.int32)[:, None]
        + offset
        + jnp.arange(count, dtype=jnp.int32)[None, :]
    ) % rows
    return block[index]


def shards(inputs, w_first, w_second, requests, slots, counts, edge_weight, offsets):
    rows = inputs.shape[0]
    width = w_second.shape[1]
    peers = lax.axis_size("wide")
    total_rows = rows * peers * lax.axis_size("narrow")
    pre, hidden, codes = forward(inputs, w_first, w_second)
    sent = codes.astype(jnp.bfloat16)
    asked = lax.all_to_all(requests, "wide", split_axis=0, concat_axis=0, tiled=True)
    found = jnp.take(sent, asked.reshape(-1), axis=0).reshape(asked.shape[0], asked.shape[1], width)
    table = lax.all_to_all(found, "wide", split_axis=0, concat_axis=0, tiled=True).reshape(
        -1, width
    )
    near = jnp.take(table, slots, axis=0)
    live = jnp.arange(slots.shape[1], dtype=jnp.int32)[None, :] < counts[:, None]
    weight = jnp.where(live, edge_weight.astype(jnp.float32), jnp.float32(0.0))
    grad = attract(codes, near, weight)
    block = sent
    for step in range(offsets.shape[0]):
        block = from_behind(block, "narrow", 1)
        grad = grad + repel(codes, negatives(block, offsets[step], NEGW))
    scale = 2.0 / (slots.shape[1] * math.sqrt(total_rows))
    dcodes = (scale * grad).astype(jnp.bfloat16)
    part_second = jnp.dot(hidden.T, dcodes, preferred_element_type=jnp.float32)
    dhidden = jnp.dot(dcodes, w_second.T, preferred_element_type=jnp.float32)
    dpre = jnp.where(pre > 0, dhidden, jnp.float32(0.0)).astype(jnp.bfloat16)
    part_first = jnp.dot(inputs.T, dpre, preferred_element_type=jnp.float32)
    owned = sent_together((part_first, part_second), "wide", 0, 1)
    grad_first, grad_second = in_one((owned[0], owned[1]), "narrow")
    return (grad_first, grad_second)


def solution(mesh):
    return jax.shard_map(
        shards,
        mesh=mesh,
        in_specs=(
            P(("wide", "narrow"), None),
            P(),
            P(),
            P(("wide", "narrow"), None),
            P(("wide", "narrow"), None),
            P(("wide", "narrow")),
            P(("wide", "narrow"), None),
            P(),
        ),
        out_specs=(P("wide", None), P("wide", None)),
        check_vma=False,
    )
```

profile of v0, /device:TPU:32, one launch (start us, length us, event | category | flops | bytes accessed | tf_op | source)
XLA Modules:
  0.0 474.3 jit_solution(11268964839031993153)
XLA Ops:
  7.2 1.6 copy-done
  8.8 2.5 fusion.52
  11.3 1.5 fusion.51
  12.7 1.6 collective-permute-start
  14.3 10.1 %all-to-all-start = ((s32[16,1,128]{2,1,0:T(1,128)}), s32[16,1,128]{2,1,0:T(1,128)S(1)}, u32[]{:S(2)}, u32[]{:S(2)}) async-start(s32[16,1,128]{2,1,0:T(1,128)} %bitcast), calls=%async_computation | async-start | bytes 16384 | tf_op jit(solution)/shard_map/all_to_all | solution.py:84
  24.5 0.7 fusion.50
  25.2 0.7 iota_add_fusion.3
  26.2 0.7 iota_add_fusion
  27.3 0.6 iota_add_fusion.1
  28.2 0.7 iota_add_fusion.2
  29.6 0.8 copy.44
  30.4 0.8 copy.43
  31.2 3.1 all-to-all-done
  34.4 1.7 collective-permute-start.1
  36.0 9.0 %gather_fusion = bf16[2048,256]{1,0:T(8,128)(2,1)} fusion(bf16[512,256]{1,0:T(8,128)(2,1)S(1)} %get-tuple-element.13, s32[2048]{0:T(1024)S(1)} %broadcast_clamp_fusion.4), kind=kCustom, calls=%fused_computation | custom fusion | bytes 2105344 | tf_op jit(solution)/shard_map/jit(_take)/gather | solution.py:85
  45.0 1.4 collective-permute-start.2
  46.4 2.3 broadcast_select_fusion.1
  48.7 6.5 %all-to-all-start.1 = ((bf16[16,128,256]{2,1,0:T(8,128)(2,1)}), bf16[16,128,256]{2,1,0:T(8,128)(2,1)S(1)}, u32[]{:S(2)}, u32[]{:S(2)}) async-start(bf16[16,128,256]{2,1,0:T(8,128)(2,1)} %broadcast_select_fusion.1), calls=%async_computation.1 | async-start | bytes 2097152 | tf_op jit(solution)/shard_map/all_to_all | solution.py:86
  55.3 16.9 %gather_fusion.2 = bf16[4096,256]{1,0:T(8,128)(2,1)} fusion(bf16[512,256]{1,0:T(8,128)(2,1)S(1)} %collective-permute-done, s32[4096]{0:T(1024)S(1)} %broadcast_clamp_fusion.3), kind=kCustom, calls=%fused_computation.2 | custom fusion | bytes 4210688 | tf_op jit(solution)/shard_map/gather | solution.py:74
  72.2 0.7 collective-permute-start.3
  72.9 3.0 fusion.14
  75.9 1.0 copy.46
  77.0 0.8 copy.47
  77.8 16.8 %gather_fusion.3 = bf16[4096,256]{1,0:T(8,128)(2,1)} fusion(bf16[512,256]{1,0:T(8,128)(2,1)} %collective-permute-done.1, s32[4096]{0:T(1024)S(1)} %broadcast_clamp_fusion.2), kind=kCustom, calls=%fused_computation.3 | custom fusion | bytes 4210688 | tf_op jit(solution)/shard_map/gather | solution.py:74
  94.7 16.8 %gather_fusion.4 = bf16[4096,256]{1,0:T(8,128)(2,1)} fusion(bf16[512,256]{1,0:T(8,128)(2,1)} %collective-permute-done.2, s32[4096]{0:T(1024)S(1)} %broadcast_clamp_fusion.1), kind=kCustom, calls=%fused_computation.4 | custom fusion | bytes 4210688 | tf_op jit(solution)/shard_map/gather | solution.py:74
  111.5 16.9 %gather_fusion.5 = bf16[4096,256]{1,0:T(8,128)(2,1)} fusion(bf16[512,256]{1,0:T(8,128)(2,1)S(1)} %collective-permute-done.3, s32[4096]{0:T(1024)S(1)} %broadcast_clamp_fusion), kind=kCustom, calls=%fused_computation.5 | custom fusion | bytes 4210688 | tf_op jit(solution)/shard_map/gather | solution.py:74
  128.4 8.7 %fusion.15 = (f32[512,256]{1,0:T(8,128)}, f32[512,8]{1,0:T(8,128)S(1)}, f32[512,8]{1,0:T(8,128)}, f32[512,8]{1,0:T(8,128)}) fusion(bf16[4096,256]{1,0:T(8,128)(2,1)} %gather_fusion.2, f32[512,8]{1,0:T(8,128)} %copy.47, f32[512,256]{1,0:T(8,128)} %get-tuple-element.14, bf16[4096,256]{1,0:T(8,128)(2,1)} %gather_fusion.3, bf16[4096,256]{1,0:T(8,128)(2,1)} %gather_fusion.4, ...), kind=kLoop, calls=%fused_computation.29 | loop fusion | flops 16633856 | bytes 9502720 | tf_op jit(solution)/shard_map/reduce_sum | solution.py:64
  137.4 1.0 copy.50
  138.4 0.8 copy.51
  139.3 1.0 copy.52
  140.4 0.8 copy.53
  141.2 8.3 %fusion.11 = (f32[512,256]{1,0:T(8,128)}, f32[512,256]{1,0:T(8,128)}, f32[512,256]{1,0:T(8,128)}) fusion(bf16[4096,256]{1,0:T(8,128)(2,1)} %gather_fusion.3, f32[512,8]{1,0:T(8,128)S(1)} %copy.49, f32[512,256]{1,0:T(8,128)} %get-tuple-element.14, bf16[4096,256]{1,0:T(8,128)(2,1)} %gather_fusion.5, f32[512,8]{1,0:T(8,128)} %copy.53, ...), kind=kLoop, calls=%fused_computation.24 | loop fusion | flops 12189696 | bytes 8437760 | tf_op jit(solution)/shard_map/reduce_sum | solution.py:64
  149.5 22.0 %gather_fusion.1 = bf16[7680,256]{1,0:T(8,128)(2,1)} fusion(bf16[2048,256]{1,0:T(8,128)(2,1)S(1)} %bitcast.51, s32[8192]{0:T(1024)S(1)} %pad_clamp_fusion), kind=kCustom, calls=%fused_computation.1 | custom fusion | bytes 7895040 | tf_op jit(solution)/shard_map/jit(_take)/gather | solution.py:89
  171.6 6.8 %reshape.451 = bf16[512,15,256]{2,1,0:T(8,128)(2,1)} reshape(bf16[7680,256]{1,0:T(8,128)(2,1)} %gather_fusion.1) | data formatting | bytes 7864320 | tf_op jit(solution)/shard_map/jit(_take)/gather | solution.py:89
  178.4 15.3 %multiply_reduce_fusion.1 = f32[512,15]{1,0:T(8,128)S(1)} fusion(f32[512,256]{1,0:T(8,128)S(1)} %copy-done.2, bf16[512,15,256]{2,1,0:T(8,128)(2,1)} %reshape.451, pred[512,15]{1,0:T(8,128)(4,1)S(1)} %copy-done.11), kind=kLoop, calls=%fused_computation.7 | loop fusion | flops 9822720 | bytes 4494848 | tf_op jit(solution)/shard_map/reduce_sum | solution.py:55
  194.0 3.3 multiply_reduce_fusion
  197.5 5.4 %convolution_bitcast_fusion = f32[1024,1024]{0,1:T(8,128)} fusion(bf16[512,1024]{1,0:T(8,128)(2,1)} %param.8, f32[512,1024]{1,0:T(8,128)} %copy-done.3, bf16[512,256]{1,0:T(8,128)(2,1)S(1)} %multiply_convert_fusion, bf16[1024,256]{1,0:T(8,128)(2,1)S(1)} %copy-done.5), kind=kOutput, calls=%fused_computation.31 | convolution fusion | flops 1343750144 | bytes 8126464 | tf_op jit(solution)/shard_map/dot_general | solution.py:102
  202.9 2.1 fusion.17
  205.0 5.4 %pad_maximum_fusion = f32[1024,1280]{0,1:T(8,128)} fusion(f32[1024,256]{0,1:T(8,128)S(1)} %fusion.17, f32[1024,1024]{0,1:T(8,128)} %convolution_bitcast_fusion), kind=kLoop, calls=%fused_computation.9 | loop fusion | flops 1310720 | bytes 10485760 | tf_op jit(solution)/shard_map/concatenate | solution.py:22
  210.4 6.0 %copy.57 = f32[1024,1280]{1,0:T(8,128)} copy(f32[1024,1280]{0,1:T(8,128)} %pad_maximum_fusion) | data formatting | bytes 10485760
  216.3 114.3 %reduce-scatter.4.cloned.1.call-done = f32[64,1280]{1,0:T(8,128)} async-done(((f32[1024,1280]{1,0:T(8,128)}), f32[64,1280]{1,0:T(8,128)}) %reduce-scatter.4.cloned.1.call-update) | async-done | bytes 327696
  330.6 1.0 slice_bitcast_fusion
  331.7 0.8 slice_bitcast_fusion.1
  332.6 6.4 %broadcast_in_dim.35 = f32[16,1,81920]{2,1,0:T(1,128)} broadcast(f32[81920]{0:T(1024)S(1)} %pad_maximum_fusion.1), dimensions={2} | broadcast | bytes 5570560 | tf_op jit(solution)/shard_map/broadcast_in_dim | solution.py:29
  338.9 121.2 %all_to_all.20 = f32[16,1,81920]{2,1,0:T(1,128)} all-to-all(f32[16,1,81920]{2,1,0:T(1,128)} %broadcast_in_dim.35), channel_id=1, replica_groups=mesh['wide'=16,'narrow'=16] {'narrow'}, dimensions={0} | all-to-all | bytes 10485760 | tf_op jit(solution)/shard_map/all_to_all | solution.py:30
  460.1 5.9 %reduce_sum.109 = f32[81920]{0:T(1024)S(1)} reduce(f32[16,1,81920]{2,1,0:T(1,128)} %all_to_all.20, f32[]{:T(128)} %constant.66.clone.1), dimensions={0,1}, to_apply=%region_11.12 | reduce | flops 1228800 | bytes 5570564 | tf_op jit(solution)/shard_map/reduce_sum | solution.py:34
  466.1 0.7 slice.43
  466.8 0.6 slice.45
  (72 shorter events, 2.7 us)
Async XLA Ops:
  7.2 1.6 copy-start
  7.2 4.1 copy-start.4
  7.2 17.3 %copy-start.12 = (s32[512,15]{0,1:T(8,128)S(1)}, s32[512,15]{0,1:T(8,128)}, u32[]{:S(2)}) copy-start(s32[512,15]{0,1:T(8,128)} %param.12) | copy-start | bytes 92164
  7.2 17.3 %copy-start.14 = (s32[4]{0:T(128)S(1)}, s32[4]{0:T(128)}, u32[]{:S(2)}) copy-start(s32[4]{0:T(128)} %param.15) | copy-start | bytes 52
  11.2 1.5 copy-start.3
  11.3 19.1 %copy-start.13 = (s32[512,15]{0,1:T(8,128)S(1)}, s32[512,15]{0,1:T(8,128)}, u32[]{:S(2)}) copy-start(s32[512,15]{0,1:T(8,128)} %param.14) | copy-start | bytes 92164
  12.7 21.6 %collective-permute-start = (bf16[512,256]{1,0:T(8,128)(2,1)S(1)}, bf16[512,256]{1,0:T(8,128)(2,1)S(1)}, u32[]{:S(2)}, u32[]{:S(2)}) collective-permute-start(bf16[512,256]{1,0:T(8,128)(2,1)S(1)} %get-tuple-element.13), channel_id=1, source_target_pairs={{15,0},{0,1},{1,2},{2,3},{3,4},{4,5},{5,6},{6,7},{7,8},{8,9},{9,10... | collective-permute-start | bytes 786440 | tf_op jit(solution)/shard_map/ppermute | solution.py:14
  14.3 20.0 %all-to-all-start = ((s32[16,1,128]{2,1,0:T(1,128)}), s32[16,1,128]{2,1,0:T(1,128)S(1)}, u32[]{:S(2)}, u32[]{:S(2)}) async-start(s32[16,1,128]{2,1,0:T(1,128)} %bitcast), calls=%async_computation | async-start | bytes 16384 | tf_op jit(solution)/shard_map/all_to_all | solution.py:84
  34.4 10.7 %collective-permute-start.1 = (bf16[512,256]{1,0:T(8,128)(2,1)S(1)}, bf16[512,256]{1,0:T(8,128)(2,1)}, u32[]{:S(2)}, u32[]{:S(2)}) collective-permute-start(bf16[512,256]{1,0:T(8,128)(2,1)S(1)} %collective-permute-done), channel_id=1, source_target_pairs={{15,0},{0,1},{1,2},{2,3},{3,4},{4,5},{5,6},{6,7},{7,8},{8,9},{9,10... | collective-permute-start | bytes 786440 | tf_op jit(solution)/shard_map/ppermute | solution.py:14
  45.0 27.2 %collective-permute-start.2 = (bf16[512,256]{1,0:T(8,128)(2,1)}, bf16[512,256]{1,0:T(8,128)(2,1)}, u32[]{:S(2)}, u32[]{:S(2)}) collective-permute-start(bf16[512,256]{1,0:T(8,128)(2,1)} %collective-permute-done.1), channel_id=1, source_target_pairs={{15,0},{0,1},{1,2},{2,3},{3,4},{4,5},{5,6},{6,7},{7,8},{8,9},{9,10... | collective-permute-start | bytes 786440 | tf_op jit(solution)/shard_map/ppermute | solution.py:14
  48.7 100.8 %all-to-all-start.1 = ((bf16[16,128,256]{2,1,0:T(8,128)(2,1)}), bf16[16,128,256]{2,1,0:T(8,128)(2,1)S(1)}, u32[]{:S(2)}, u32[]{:S(2)}) async-start(bf16[16,128,256]{2,1,0:T(8,128)(2,1)} %broadcast_select_fusion.1), calls=%async_computation.1 | async-start | bytes 2097152 | tf_op jit(solution)/shard_map/all_to_all | solution.py:86
  55.3 275.4 %reduce-scatter.4.cloned.1.call-start = ((), (), s32[]{:S(2)}) async-start(), calls=%async_computation.4 | async-start | bytes 5570560
  72.2 39.2 %collective-permute-start.3 = (bf16[512,256]{1,0:T(8,128)(2,1)}, bf16[512,256]{1,0:T(8,128)(2,1)S(1)}, u32[]{:S(2)}, u32[]{:S(2)}) collective-permute-start(bf16[512,256]{1,0:T(8,128)(2,1)} %collective-permute-done.2), channel_id=1, source_target_pairs={{15,0},{0,1},{1,2},{2,3},{3,4},{4,5},{5,6},{6,7},{7,8},{8,9},{9,10... | collective-permute-start | bytes 786440 | tf_op jit(solution)/shard_map/ppermute | solution.py:14
  171.6 6.8 %copy-start.2 = (f32[512,256]{1,0:T(8,128)S(1)}, f32[512,256]{1,0:T(8,128)}, u32[]{:S(2)}) copy-start(f32[512,256]{1,0:T(8,128)} %get-tuple-element.14) | copy-start | bytes 1572868
  171.6 6.8 %copy-start.11 = (pred[512,15]{1,0:T(8,128)(4,1)S(1)}, pred[512,15]{1,0:T(8,128)(4,1)}, u32[]{:S(2)}) copy-start(pred[512,15]{1,0:T(8,128)(4,1)} %copy.44) | copy-start | bytes 23044
  178.4 15.4 %copy-start.10 = (f32[512,15]{1,0:T(8,128)S(1)}, f32[512,15]{1,0:T(8,128)}, u32[]{:S(2)}) copy-start(f32[512,15]{1,0:T(8,128)} %copy.43) | copy-start | bytes 92164
  178.4 15.3 %copy-start.15 = (s32[512]{0:T(512)S(1)}, s32[512]{0:T(512)}, u32[]{:S(2)}) copy-start(s32[512]{0:T(512)} %param.13) | copy-start | bytes 6148
  178.4 15.5 %copy-start.1 = (bf16[512,15,256]{2,1,0:T(8,128)(2,1)S(1)}, bf16[512,15,256]{2,1,0:T(8,128)(2,1)}, u32[]{:S(2)}) copy-start(bf16[512,15,256]{2,1,0:T(8,128)(2,1)} %reshape.451) | copy-start | bytes 11796484
  193.8 3.5 copy-start.6
  193.8 3.5 copy-start.7
  193.8 3.5 copy-start.8
  193.8 3.5 copy-start.9
  194.0 3.5 copy-start.5
Sparse Core Ops, SparseCore 0:
  216.5 114.1 reduce-scatter.3
where the time goes:
time: 476 us; the launch traced here: 474 us
  local copies, waits for them, and re-layouts  132 us (28%)
  blocking collectives  121 us (25%)
  waiting for transfers between devices  117 us (25%)
  other arithmetic  56.1 us (12%)
  starting transfers between devices  22 us (5%)
  between operations  14.5 us (3%)
  matrix products  11.4 us (2%)
    all_to_all x1, blocking collectives, sent_to_all(): return lax.all_to_all(copies, axis, split_axis=0, concat_axis=0, tiled=True)  121 us
    unnamed x2, waiting for transfers between devices  114 us
    gather x4, local copies, waits for them, and re-layouts, negatives(): return block[index]  67.5 us
    gather x2, local copies, waits for them, and re-layouts, shards(): near = jnp.take(table, slots, axis=0)  28.9 us
    reduce_sum x2, other arithmetic, repel(): return -jnp.sum(coef[:, :, None] * diff, axis=1)  17.1 us
    reduce_sum x1, other arithmetic, attract(): dist = jnp.sum(diff * diff, axis=-1) / diff.shape[-1]  15.3 us
    all_to_all x1, starting transfers between devices, shards(): lax.all_to_all(requests, 'wide', split_axis=0, concat_axis=0, tiled=True)  10.1 us
  transfers between devices with their start and end apart: 7, of which 2 were waited for; matrix products, arithmetic and copies ran while one was open for 24% of the time, Pallas kernels for 0%

commit v1 on v0

v1 whole, which is shorter than its diff:
```python
import math

import jax
import jax.numpy as jnp
from jax import lax
from jax.experimental import pallas as pl
from jax.experimental.pallas import tpu as pltpu
from jax.sharding import PartitionSpec as P

MESH = pl.DeviceIdType.MESH
F32 = jnp.float32
BF16 = jnp.bfloat16
NEGW = 8
NX, NH, NC, NL, NY = 4, 2, 2, 4, 4


def nt(a, b):
    return lax.dot_general(a, b, (((1,), (1,)), ((), ())), preferred_element_type=F32)


def nn(a, b):
    return jnp.dot(a, b, preferred_element_type=F32)


def step(
    scale, inputs, w1, w2, requests, slots, counts, edges, offsets, out_first, out_second,
    hidden, codes, sent, mate, far, reqs, asked, keys, found, table, weights, norms,
    xt, ht, sums, acc, dist, coef, dpre, dcodes, ga, gb,
    ca_out, ca_in, cb_out, cb_in, pa1_out, pa1_in, pb1_out, pb1_in, fa1, fb1,
    pa2_out, pa2_in, pb2_out, pb2_in, zs_out, zs_in, whole, send_sem, recv_sem,
):
    w = lax.axis_index("wide")
    n = lax.axis_index("narrow")
    x, h, c = w // 4, (w // 2) % 2, w % 2
    l, y = n // 4, n % 4
    rows = inputs.shape[0]
    sem_count = [0]

    def device(xx, hh, cc, ll, yy):
        return (xx * 4 + hh * 2 + cc, ll * 4 + yy)

    def copy(src, dst, target):
        at = sem_count[0]
        sem_count[0] += 1
        return pltpu.make_async_remote_copy(
            src_ref=src, dst_ref=dst, send_sem=send_sem.at[at], recv_sem=recv_sem.at[at],
            device_id=target, device_id_type=MESH,
        )

    def xs(s):
        return (x + s) % NX

    def ys(s):
        return (y + s) % NY

    def ls(s):
        return (l + s) % NL

    barrier = pltpu.get_barrier_semaphore()
    plane = [(dx, dc) for dx in range(NX) for dc in range(NC) if dx or dc]
    ring = [(dl, dy) for dl in range(NL) for dy in range(NY) if dl or dy]
    peers = [device(xs(dx), h, (c + dc) % 2, l, y) for dx, dc in plane]
    peers += [device(x, h, c, ls(dl), ys(dy)) for dl, dy in ring]
    peers += [device(x, 1 - h, c, ls(dl), y) for dl in range(NL)]
    for peer in peers:
        pl.semaphore_signal(barrier, inc=1, device_id=peer, device_id_type=MESH)

    reqs[...] = jnp.zeros_like(reqs)
    for xx in range(NX):
        for cc in range(NC):
            for hh in range(NH):
                p = xx * 4 + hh * 2 + cc
                reqs[xx * 2 + cc, hh : hh + 1, :] = requests[p : p + 1, :]

    for at in range(0, 1024, 256):
        pre = nn(inputs[...], w1[:, at : at + 256])
        hidden[:, at : at + 256] = jnp.maximum(pre, 0.0).astype(BF16)
    codes[...] = nn(hidden[...], w2[...])
    sent[...] = codes[...].astype(BF16)

    pl.semaphore_wait(barrier, len(peers))

    ask = []
    for dx, dc in plane:
        j = dx * 2 + dc
        cp = copy(reqs.at[xs(dx) * 2 + (c + dc) % 2], asked.at[j], device(xs(dx), h, (c + dc) % 2, l, y))
        cp.start()
        ask.append(cp)
    to_next = copy(sent, far.at[3], device(x, h, c, ls(1), y))
    to_next.start()
    to_mate = copy(sent, mate, device(x, 1 - h, c, l, y))
    to_mate.start()
    to_y = []
    for s in (1, 2, 3):
        cp = copy(sent, far.at[s - 1], device(x, h, c, l, ys(s)))
        to_y.append(cp)
        pl.when(y + s < NY)(cp.start)

    live = lax.broadcasted_iota(jnp.int32, slots.shape, 0) < counts[...]
    keys[...] = jnp.zeros_like(keys)
    keys[0:15, :] = slots[...].astype(F32)
    keys[16:31, :] = jnp.where(live, edges[...], 0).astype(F32)
    norms[...] = keys[...].T

    def weigh(at, _):
        r = pl.multiple_of(at * 16, 16)
        both = norms[pl.ds(r, 16), :]
        lane = lax.broadcasted_iota(jnp.int32, (16, 512), 1).astype(F32)
        spots = [jnp.broadcast_to(both[:, k : k + 1], (16, 512)) for k in range(15)]
        worth = [jnp.broadcast_to(both[:, 16 + k : 17 + k], (16, 512)) for k in range(15)]
        for part in range(4):
            total = jnp.zeros((16, 512), F32)
            for k in range(15):
                total = total + jnp.where(spots[k] == lane + float(part * 512), worth[k], 0.0)
            weights[part, pl.ds(r, 16), :] = total.astype(BF16)
        return 0

    lax.fori_loop(0, rows // 32, weigh, 0)

    for cp in ask:
        cp.wait_recv()
    asked[0] = reqs[x * 2 + c]
    for j in range(8):
        norms2 = asked[j]
        keys[j * 8 : j * 8 + 8, 0:128] = norms2.astype(F32)
    wanted = keys[:, 0:128].T

    reply = []

    def serve(block, b):
        lane = lax.broadcasted_iota(jnp.int32, (128, rows), 1).astype(F32)
        for j in (2, 6, 4, 3, 7, 5, 1, 0):
            dx, dc = j // 2, j % 2
            col = j * 8
            which = jnp.where(b == 0, wanted[:, col : col + 1], wanted[:, col + 1 : col + 2])
            pick = jnp.where(jnp.broadcast_to(which, (128, rows)) == lane, 1.0, 0.0).astype(BF16)
            got = nn(pick, block[...]).astype(BF16)
            if j == 0:
                table[x, pl.ds(pl.multiple_of(b * 256 + c * 128, 128), 128), :] = got
            else:
                slot = (j - 1) * 2
                found[slot + (0 if block is sent else 1)] = got
                cp = copy(
                    found.at[slot + (0 if block is sent else 1)],
                    table.at[x, pl.ds(pl.multiple_of(b * 256 + c * 128, 128), 128), :],
                    device(xs(NX - dx), h, (c + dc) % 2, l, y),
                )
                cp.start()
                reply.append((dx, cp))

    serve(sent, h)
    to_next.wait_recv()
    for s in (1, 2, 3):
        cp = pltpu.make_async_remote_copy(
            src_ref=far.at[3], dst_ref=far.at[s - 1], send_sem=send_sem.at[9 + s - 1],
            recv_sem=recv_sem.at[9 + s - 1], device_id=device(x, h, c, l, ys(s)), device_id_type=MESH,
        )
        pl.when(y + s >= NY)(cp.start)
    lax.fori_loop(rows // 32, rows // 16, weigh, 0)
    for g in range(8):
        xt[g * 128 : g * 128 + 128, :] = inputs[:, g * 128 : g * 128 + 128].T
        ht[g * 128 : g * 128 + 128, :] = hidden[:, g * 128 : g * 128 + 128].T
    to_mate.wait_recv()
    serve(mate, 1 - h)

    own = sent[...].astype(F32)
    norm = jnp.sum(own * own, axis=1, keepdims=True)
    norms[...] = jnp.broadcast_to(norm, norms.shape)
    sums[...] = jnp.zeros_like(sums)
    acc[...] = jnp.zeros_like(acc)
    ones = jnp.ones((8, 256), BF16)
    inv = 1.0 / 256.0

    def squares(block):
        z = block.astype(F32)
        z = z * z
        hi = z.astype(BF16)
        lo = (z - hi.astype(F32)).astype(BF16)
        return (nt(ones, hi) + nt(ones, lo))[0:1, :]

    def pull(block, part, kind, offset):
        dist[...] = nt(sent[...], block)
        size = squares(block)

        def tile(at, _):
            r = pl.multiple_of(at * 32, 32)
            mine = norms[pl.ds(r, 32), :]
            total = sums[pl.ds(r, 32), :]
            for q in range(4):
                cols = slice(q * 128, q * 128 + 128)
                d = jnp.maximum((mine + size[:, cols]) - 2.0 * dist[pl.ds(r, 32), cols], 0.0) * inv
                if kind == "near":
                    k = weights[part, pl.ds(r, 32), cols].astype(F32) / (1.0 + d)
                else:
                    i = lax.broadcasted_iota(jnp.int32, (32, 128), 0)
                    j = lax.broadcasted_iota(jnp.int32, (32, 128), 1)
                    band = ((j - i) + (q * 128 - r - offset)) & (rows - 1)
                    k = jnp.where(band < NEGW, -1.0 / ((1.0 + d) * (1.1 * d + 0.1)), 0.0)
                k = k.astype(BF16)
                coef[pl.ds(r, 32), cols] = k
                total = total + k.astype(F32)
            sums[pl.ds(r, 32), :] = total
            return 0

        lax.fori_loop(0, rows // 32, tile, 0)
        acc[...] += nn(coef[...], block)

    pull(far[3], None, "far", offsets[3])
    for s in (1, 3, 2):
        to_y[s - 1].wait_recv()
        pull(far[s - 1], None, "far", offsets[s - 1])
    for dx in (0, 1, 3, 2):
        for at, cp in reply:
            if at == dx:
                cp.wait_recv()
        part = xs(dx)
        pull(table[part], part, "near", None)

    total = jnp.sum(sums[...], axis=1, keepdims=True)
    dcodes[...] = (scale * (total * codes[...] - acc[...])).astype(BF16)

    core = device(x, h, 1 - c, l, y)
    second = nn(ht[...], dcodes[...])
    ga[:, 512:640] = second[:, 0:128]
    gb[:, 512:640] = second[:, 128:256]

    def backward(g, first):
        for at in range(first, first + 512, 256):
            back = nt(dcodes[...], w2[at : at + 256, :])
            dpre[:, at : at + 256] = jnp.where(hidden[:, at : at + 256] > 0, back, 0.0).astype(BF16)
            g[:, at - first : at - first + 256] = nn(xt[...], dpre[:, at : at + 256])

    def part_rows(xx, hh, cc, yy):
        return pl.ds(pl.multiple_of(xx * 256 + hh * 128 + cc * 64 + yy * 16, 16), 16)

    backward(gb, 512)
    for xx in range(NX):
        for hh in range(NH):
            for yy in range(NY):
                cb_out[yy, xx, hh] = gb[part_rows(xx, hh, 1 - c, yy), :].astype(BF16)
    core_b = copy(cb_out, cb_in, core)
    core_b.start()
    backward(ga, 0)
    for xx in range(NX):
        for hh in range(NH):
            for yy in range(NY):
                ca_out[xx, hh, yy] = ga[part_rows(xx, hh, 1 - c, yy), :].astype(BF16)
    core_a = copy(ca_out, ca_in, core)
    core_a.start()

    core_b.wait_recv()
    for yy in range(NY):
        for xx in range(NX):
            for hh in range(NH):
                both = gb[part_rows(xx, hh, c, yy), :] + cb_in[yy, xx, hh].astype(F32)
                pb1_out[yy, xx, hh] = both.astype(BF16)
    b1 = []
    for s in (1, 2, 3):
        cp = copy(pb1_out.at[ys(s)], pb1_in.at[s - 1], device(x, h, c, l, ys(s)))
        cp.start()
        b1.append(cp)
    core_a.wait_recv()
    for xx in range(NX):
        for hh in range(NH):
            for yy in range(NY):
                both = ga[part_rows(xx, hh, c, yy), :] + ca_in[xx, hh, yy].astype(F32)
                pa1_out[xx, hh, yy] = both.astype(BF16)
    a1 = []
    for s in (1, 2, 3):
        cp = copy(pa1_out.at[xs(s)], pa1_in.at[s - 1], device(xs(s), h, c, l, y))
        cp.start()
        a1.append(cp)
    for xx in range(NX):
        for hh in range(NH):
            fb1[xx, hh] = gb[part_rows(xx, hh, c, y), :] + cb_in[y, xx, hh].astype(F32)
    for hh in range(NH):
        for yy in range(NY):
            fa1[yy, hh] = ga[part_rows(x, hh, c, yy), :] + ca_in[x, hh, yy].astype(F32)

    for cp in b1:
        cp.wait_recv()
    for xx in range(NX):
        for hh in range(NH):
            got = [pb1_in[s, xx, hh].astype(F32) for s in range(3)]
            fb1[xx, hh] += got[0] + got[1] + got[2]
            pb2_out[xx, hh] = fb1[xx, hh].astype(BF16)
    b2 = []
    for s in (1, 2, 3):
        cp = copy(pb2_out.at[xs(s)], pb2_in.at[s - 1], device(xs(s), h, c, l, y))
        cp.start()
        b2.append(cp)
    for cp in a1:
        cp.wait_recv()
    for yy in range(NY):
        for hh in range(NH):
            got = [pa1_in[s, hh, yy].astype(F32) for s in range(3)]
            fa1[yy, hh] += got[0] + got[1] + got[2]
            pa2_out[yy, hh] = fa1[yy, hh].astype(BF16)
    a2 = []
    for s in (1, 2, 3):
        cp = copy(pa2_out.at[ys(s)], pa2_in.at[s - 1], device(x, h, c, l, ys(s)))
        cp.start()
        a2.append(cp)
    for cp in b2 + a2:
        cp.wait_recv()
    for hh in range(NH):
        for half, mine, got in ((0, fa1[y, hh], pa2_in), (1, fb1[x, hh], pb2_in)):
            total = mine + got[0, hh].astype(F32) + got[1, hh].astype(F32) + got[2, hh].astype(F32)
            zs_out[hh, half] = total[0:8, :]
            zs_out[hh, 2 + half] = total[8:16, :]

    zs = []
    for dh in range(NH):
        for dl in range(NL):
            if dh or dl:
                hh = (h + dh) % 2
                cp = copy(zs_out.at[hh, ls(dl)], zs_in.at[dh * 4 + dl], device(x, hh, c, ls(dl), y))
                cp.start()
                zs.append(cp)
    total = zs_out[h, l]
    for cp in zs:
        cp.wait_recv()
    for j in range(1, 8):
        total = total + zs_in[j]
    whole[y, l] = total
    spread = []
    for dl, dy in ring:
        cp = copy(whole.at[y, l], whole.at[y, l], device(x, h, c, ls(dl), ys(dy)))
        cp.start()
        spread.append(cp)
    for cp in spread:
        cp.wait_recv()
    for yy in range(NY):
        for ll in range(NL):
            r = yy * 16 + (ll // 2) * 8
            half = ll % 2
            out_first[r : r + 8, half * 512 : half * 512 + 512] = whole[yy, ll, :, 0:512]
            out_second[r : r + 8, half * 128 : half * 128 + 128] = whole[yy, ll, :, 512:640]

    for cp in ask + [to_next, to_mate] + to_y + [cp for _, cp in reply] + [core_a, core_b]:
        cp.wait_send()
    for cp in a1 + b1 + a2 + b2 + zs + spread:
        cp.wait_send()


def shards(inputs, w_first, w_second, requests, slots, counts, edge_weight, offsets):
    rows = inputs.shape[0]
    total_rows = rows * lax.axis_size("wide") * lax.axis_size("narrow")
    scale = 2.0 / (slots.shape[1] * math.sqrt(total_rows))
    vmem = pl.BlockSpec(memory_space=pltpu.VMEM)
    smem = pl.BlockSpec(memory_space=pltpu.SMEM)
    return pl.pallas_call(
        lambda *refs: step(scale, *refs),
        out_shape=(jax.ShapeDtypeStruct((64, 1024), F32), jax.ShapeDtypeStruct((64, 256), F32)),
        in_specs=[vmem] * 7 + [smem],
        out_specs=(vmem, vmem),
        scratch_shapes=[
            pltpu.VMEM((512, 1024), BF16),
            pltpu.VMEM((512, 256), F32),
            pltpu.VMEM((512, 256), BF16),
            pltpu.VMEM((512, 256), BF16),
            pltpu.VMEM((4, 512, 256), BF16),
            pltpu.VMEM((8, 8, 128), jnp.int32),
            pltpu.VMEM((8, 8, 128), jnp.int32),
            pltpu.VMEM((128, 512), F32),
            pltpu.VMEM((14, 128, 256), BF16),
            pltpu.VMEM((4, 512, 256), BF16),
            pltpu.VMEM((4, 512, 512), BF16),
            pltpu.VMEM((512, 128), F32),
            pltpu.VMEM((1024, 512), BF16),
            pltpu.VMEM((1024, 512), BF16),
            pltpu.VMEM((512, 128), F32),
            pltpu.VMEM((512, 256), F32),
            pltpu.VMEM((512, 512), F32),
            pltpu.VMEM((512, 512), BF16),
            pltpu.VMEM((512, 1024), BF16),
            pltpu.VMEM((512, 256), BF16),
            pltpu.VMEM((1024, 640), F32),
            pltpu.VMEM((1024, 640), F32),
            pltpu.VMEM((4, 2, 4, 16, 640), BF16),
            pltpu.VMEM((4, 2, 4, 16, 640), BF16),
            pltpu.VMEM((4, 4, 2, 16, 640), BF16),
            pltpu.VMEM((4, 4, 2, 16, 640), BF16),
            pltpu.VMEM((4, 2, 4, 16, 640), BF16),
            pltpu.VMEM((3, 2, 4, 16, 640), BF16),
            pltpu.VMEM((4, 4, 2, 16, 640), BF16),
            pltpu.VMEM((3, 4, 2, 16, 640), BF16),
            pltpu.VMEM((4, 2, 16, 640), F32),
            pltpu.VMEM((4, 2, 16, 640), F32),
            pltpu.VMEM((4, 2, 16, 640), BF16),
            pltpu.VMEM((3, 2, 16, 640), BF16),
            pltpu.VMEM((4, 2, 16, 640), BF16),
            pltpu.VMEM((3, 2, 16, 640), BF16),
            pltpu.VMEM((2, 4, 8, 640), F32),
            pltpu.VMEM((8, 8, 640), F32),
            pltpu.VMEM((4, 4, 8, 640), F32),
            pltpu.SemaphoreType.DMA((64,)),
            pltpu.SemaphoreType.DMA((64,)),
        ],
        compiler_params=pltpu.CompilerParams(
            collective_id=0, has_side_effects=True, vmem_limit_bytes=56 << 20
        ),
        cost_estimate=pl.CostEstimate(flops=9_000_000_000, bytes_accessed=5_000_000, transcendentals=0),
        name="embedding_step",
    )(
        inputs, w_first, w_second, requests, slots.T, counts.reshape(1, -1), edge_weight.T, offsets
    )


def solution(mesh):
    return jax.shard_map(
        shards,
        mesh=mesh,
        in_specs=(
            P(("wide", "narrow"), None),
            P(),
            P(),
            P(("wide", "narrow"), None),
            P(("wide", "narrow"), None),
            P(("wide", "narrow")),
            P(("wide", "narrow"), None),
            P(),
        ),
        out_specs=(P("wide", None), P("wide", None)),
        check_vma=False,
    )
```

time: 476 us -> 84.1 us (0.18)
  local copies, waits for them, and re-layouts: 132 us -> 3.14 us
  blocking collectives: 121 us -> 0 us
  waiting for transfers between devices: 117 us -> 0 us
  Pallas kernels: 0 us -> 80.1 us
  other arithmetic: 56.1 us -> 0 us
  starting transfers between devices: 22 us -> 0 us
  between operations: 14.5 us -> 0.64 us
  matrix products: 11.4 us -> 0 us
    all_to_all x1 -> x0, blocking collectives: 121 us -> none  [sent_to_all(): return lax.all_to_all(copies, axis, split_axis=0, concat_axis=0, tiled=True)]
    unnamed x2 -> x0, waiting for transfers between devices: 114 us -> none
    gather x7 -> x0, local copies, waits for them, and re-layouts: 105 us -> none  [the longest x4 67.5 us: negatives(): return block[index]]
    pallas_call x0 -> x1, Pallas kernels: none -> 80.1 us  [shards(): pl.pallas_call(lambda *refs: step(scale, *refs), out_shape=(jax.ShapeDtyp...]
    reduce_sum x6 -> x0, other arithmetic: 44.5 us -> none  [the longest x2 17.1 us: repel(): return -jnp.sum(coef[:, :, None] * diff, axis=1)]
    all_to_all x2 -> x0, starting transfers between devices: 16.7 us -> none  [the longest x1 10.1 us: shards(): lax.all_to_all(requests, 'wide', split_axis=0, concat_axis=0, tiled=True)]
    dot_general x4 -> x0, matrix products: 11.4 us -> none  [the longest x1 5.43 us: shards(): part_first = jnp.dot(inputs.T, dpre, preferred_element_type=jnp.float32)]
    broadcast_in_dim x2 -> x0, local copies, waits for them, and re-layouts: 6.58 us -> none  [the longest x1 6.36 us: sent_to_all(): copies = jnp.broadcast_to(value, (lax.axis_size(axis), *value.shape))]
  transfers between devices with their start and end apart: 7 -> 0, of which waited for: 2 -> 0; matrix products, arithmetic and copies ran while one was open for 24% -> 0% of each run, Pallas kernels for 0% -> 0%
where the time goes in v1:
time: 84.1 us; the launch traced here: 83.9 us
  Pallas kernels  80.1 us (95%)
  local copies, waits for them, and re-layouts  3.14 us (4%)
    pallas_call x1, Pallas kernels, shards(): pl.pallas_call(lambda *refs: step(scale, *refs), out_shape=(jax.ShapeDtyp...  80.1 us
    unnamed x2, local copies, waits for them, and re-layouts  3.14 us

profile of v1, /device:TPU:32, one launch (start us, length us, event | category | flops | bytes accessed | tf_op | source)
XLA Modules:
  0.0 83.9 jit_solution(3878664012498156866)
XLA Ops:
  0.6 80.1 %embedding_step.1 = (f32[64,1024]{1,0:T(8,128)}, f32[64,256]{1,0:T(8,128)}) custom-call(bf16[512,1024]{1,0:T(8,128)(2,1)} %refs_0_.1, bf16[1024,1024]{1,0:T(8,128)(2,1)} %refs_1_.1, bf16[1024,256]{1,0:T(8,128)(2,1)} %refs_2_.1, s32[16,128]{1,0:T(8,128)} %refs_3_.1, s32[15,512]{1,0:T(8,128)} %bitcast.3, s32[1,512]{1,0:T(1,128)} %bitcast.5, ...), custom_call_target="tpu_custom_call" | custom-call | flops 8999999488 | bytes 5000000 | tf_op jit(solution)/shard_map/embedding_step/pallas_call | solution.py:352
  80.8 1.7 %copy.12 = f32[64,1024]{1,0:T(8,128)} copy(f32[64,1024]{1,0:T(8,128)} %get-tuple-element.4) | data formatting | bytes 524288
  82.4 1.5 %copy.13 = f32[64,256]{1,0:T(8,128)} copy(f32[64,256]{1,0:T(8,128)} %get-tuple-element.5) | data formatting | bytes 131072

commit v2 on v1

--- a/solution.py
+++ b/solution.py
@@ -23,8 +23,8 @@
 
 
 def step(
-    scale, inputs, w1, w2, requests, slots, counts, edges, offsets, out_first, out_second,
-    hidden, codes, sent, mate, far, reqs, asked, keys, found, table, weights, norms,
+    scale, inputs_hbm, w1_hbm, w2_hbm, requests_hbm, slots_hbm, counts_hbm, edges_hbm, offsets, out,
+    inputs, w1, w2, requests, slots, counts, edges, in_sem, picks, sent_part, hidden, codes, sent, mate, far, reqs, asked, keys, found, table, weights, norms,
     xt, ht, sums, acc, dist, coef, dpre, dcodes, ga, gb,
     ca_out, ca_in, cb_out, cb_in, pa1_out, pa1_in, pb1_out, pb1_in, fa1, fb1,
     pa2_out, pa2_in, pb2_out, pb2_in, zs_out, zs_in, whole, send_sem, recv_sem,
@@ -36,6 +36,17 @@
     rows = inputs.shape[0]
     sem_count = [0]
 
+    loads = []
+    for at, (src, dst) in enumerate((
+        (inputs_hbm, inputs), (requests_hbm, requests),
+        (w1_hbm.at[:, 0:256], w1.at[:, 0:256]), (w1_hbm.at[:, 256:512], w1.at[:, 256:512]),
+        (w1_hbm.at[:, 512:768], w1.at[:, 512:768]), (w1_hbm.at[:, 768:1024], w1.at[:, 768:1024]),
+        (w2_hbm, w2), (slots_hbm, slots), (counts_hbm, counts), (edges_hbm, edges),
+    )):
+        load = pltpu.make_async_copy(src, dst, in_sem.at[at])
+        load.start()
+        loads.append(load)
+
     def device(xx, hh, cc, ll, yy):
         return (xx * 4 + hh * 2 + cc, ll * 4 + yy)
 
@@ -65,6 +76,7 @@
     for peer in peers:
         pl.semaphore_signal(barrier, inc=1, device_id=peer, device_id_type=MESH)
 
+    loads[1].wait()
     reqs[...] = jnp.zeros_like(reqs)
     for xx in range(NX):
         for cc in range(NC):
@@ -72,11 +84,15 @@
                 p = xx * 4 + hh * 2 + cc
                 reqs[xx * 2 + cc, hh : hh + 1, :] = requests[p : p + 1, :]
 
+    loads[0].wait()
     for at in range(0, 1024, 256):
+        loads[2 + at // 256].wait()
         pre = nn(inputs[...], w1[:, at : at + 256])
         hidden[:, at : at + 256] = jnp.maximum(pre, 0.0).astype(BF16)
+    loads[6].wait()
     codes[...] = nn(hidden[...], w2[...])
     sent[...] = codes[...].astype(BF16)
+    sent_part[...] = sent[...] * (2.0 / 256.0)
 
     pl.semaphore_wait(barrier, len(peers))
 
@@ -88,17 +104,24 @@
         ask.append(cp)
     to_next = copy(sent, far.at[3], device(x, h, c, ls(1), y))
     to_next.start()
-    to_mate = copy(sent, mate, device(x, 1 - h, c, l, y))
-    to_mate.start()
+    to_mate = []
+    for e in range(2):
+        cols = slice(e * 128, e * 128 + 128)
+        cp = copy(sent.at[:, cols], mate.at[:, cols], device(x, 1 - h, c, l, y))
+        cp.start()
+        to_mate.append(cp)
     to_y = []
     for s in (1, 2, 3):
         cp = copy(sent, far.at[s - 1], device(x, h, c, l, ys(s)))
         to_y.append(cp)
         pl.when(y + s < NY)(cp.start)
 
+    for load in loads[7:]:
+        load.wait()
     live = lax.broadcasted_iota(jnp.int32, slots.shape, 0) < counts[...]
     keys[...] = jnp.zeros_like(keys)
-    keys[0:15, :] = slots[...].astype(F32)
+    place = ((slots[...] - x * 512) & 2047) ^ (h * 256 + c * 128)
+    keys[0:15, :] = place.astype(F32)
     keys[16:31, :] = jnp.where(live, edges[...], 0).astype(F32)
     norms[...] = keys[...].T
 
@@ -125,96 +148,104 @@
         keys[j * 8 : j * 8 + 8, 0:128] = norms2.astype(F32)
     wanted = keys[:, 0:128].T
 
-    reply = []
-
-    def serve(block, b):
-        lane = lax.broadcasted_iota(jnp.int32, (128, rows), 1).astype(F32)
-        for j in (2, 6, 4, 3, 7, 5, 1, 0):
-            dx, dc = j // 2, j % 2
-            col = j * 8
-            which = jnp.where(b == 0, wanted[:, col : col + 1], wanted[:, col + 1 : col + 2])
-            pick = jnp.where(jnp.broadcast_to(which, (128, rows)) == lane, 1.0, 0.0).astype(BF16)
-            got = nn(pick, block[...]).astype(BF16)
-            if j == 0:
-                table[x, pl.ds(pl.multiple_of(b * 256 + c * 128, 128), 128), :] = got
-            else:
-                slot = (j - 1) * 2
-                found[slot + (0 if block is sent else 1)] = got
-                cp = copy(
-                    found.at[slot + (0 if block is sent else 1)],
-                    table.at[x, pl.ds(pl.multiple_of(b * 256 + c * 128, 128), 128), :],
-                    device(xs(NX - dx), h, (c + dc) % 2, l, y),
-                )
-                cp.start()
-                reply.append((dx, cp))
-
-    serve(sent, h)
+    lane = lax.broadcasted_iota(jnp.int32, (128, rows), 1).astype(F32)
+    reply = {}
+
+    def deliver(block, b, j, e):
+        cols = slice(0, 256) if e is None else slice(e * 128, e * 128 + 128)
+        got = nn(picks[b, j], block[:, cols]).astype(BF16)
+        dx, dc = j // 2, j % 2
+        spot = slice(b * 256 + dc * 128, b * 256 + dc * 128 + 128)
+        if j == 0:
+            table[0, spot, cols] = got
+        else:
+            found[b, j - 1, :, cols] = got
+            cp = copy(
+                found.at[b, j - 1, :, cols], table.at[dx, spot, cols],
+                device(xs(NX - dx), h, (c + dc) % 2, l, y),
+            )
+            cp.start()
+            reply.setdefault((b, dx), []).append(cp)
+
+    turns = (2, 6, 4, 3, 7, 5, 1, 0)
+    for b in range(2):
+        for j in turns:
+            which = jnp.where((h + b) % 2 == 0, wanted[:, j * 8 : j * 8 + 1], wanted[:, j * 8 + 1 : j * 8 + 2])
+            picks[b, j] = jnp.where(jnp.broadcast_to(which, (128, rows)) == lane, 1.0, 0.0).astype(BF16)
+            if b == 0:
+                deliver(sent, 0, j, None)
     to_next.wait_recv()
     for s in (1, 2, 3):
         cp = pltpu.make_async_remote_copy(
-            src_ref=far.at[3], dst_ref=far.at[s - 1], send_sem=send_sem.at[9 + s - 1],
-            recv_sem=recv_sem.at[9 + s - 1], device_id=device(x, h, c, l, ys(s)), device_id_type=MESH,
+            src_ref=far.at[3], dst_ref=far.at[s - 1], send_sem=send_sem.at[10 + s - 1],
+            recv_sem=recv_sem.at[10 + s - 1], device_id=device(x, h, c, l, ys(s)), device_id_type=MESH,
         )
         pl.when(y + s >= NY)(cp.start)
     lax.fori_loop(rows // 32, rows // 16, weigh, 0)
     for g in range(8):
         xt[g * 128 : g * 128 + 128, :] = inputs[:, g * 128 : g * 128 + 128].T
         ht[g * 128 : g * 128 + 128, :] = hidden[:, g * 128 : g * 128 + 128].T
-    to_mate.wait_recv()
-    serve(mate, 1 - h)
-
+
+    inv = 1.0 / 256.0
     own = sent[...].astype(F32)
     norm = jnp.sum(own * own, axis=1, keepdims=True)
-    norms[...] = jnp.broadcast_to(norm, norms.shape)
+    norms[...] = jnp.broadcast_to(norm * inv + 1.0, norms.shape)
     sums[...] = jnp.zeros_like(sums)
     acc[...] = jnp.zeros_like(acc)
     ones = jnp.ones((8, 256), BF16)
-    inv = 1.0 / 256.0
 
     def squares(block):
         z = block.astype(F32)
         z = z * z
         hi = z.astype(BF16)
         lo = (z - hi.astype(F32)).astype(BF16)
-        return (nt(ones, hi) + nt(ones, lo))[0:1, :]
-
-    def pull(block, part, kind, offset):
-        dist[...] = nt(sent[...], block)
-        size = squares(block)
+        return (nt(ones, hi) + nt(ones, lo))[0:1, :] * inv
+
+    def pull(block, dx, b, offset):
+        wide = block.shape[0]
+        dist[:, 0:wide] = nt(sent_part[...], block[...])
+        size = squares(block[...])
 
         def tile(at, _):
-            r = pl.multiple_of(at * 32, 32)
-            mine = norms[pl.ds(r, 32), :]
-            total = sums[pl.ds(r, 32), :]
-            for q in range(4):
+            r = pl.multiple_of(at * 64, 64)
+            mine = norms[pl.ds(r, 64), :]
+            total = sums[pl.ds(r, 64), :]
+            for q in range(wide // 128):
                 cols = slice(q * 128, q * 128 + 128)
-                d = jnp.maximum((mine + size[:, cols]) - 2.0 * dist[pl.ds(r, 32), cols], 0.0) * inv
-                if kind == "near":
-                    k = weights[part, pl.ds(r, 32), cols].astype(F32) / (1.0 + d)
+                d = jnp.maximum((mine + size[:, cols]) - dist[pl.ds(r, 64), cols], 1.0)
+                if dx is not None:
+                    at_b = slice(b * 256 + q * 128, b * 256 + q * 128 + 128)
+                    k = weights[dx, pl.ds(r, 64), at_b].astype(F32) * (1.0 / d)
                 else:
-                    i = lax.broadcasted_iota(jnp.int32, (32, 128), 0)
-                    j = lax.broadcasted_iota(jnp.int32, (32, 128), 1)
+                    i = lax.broadcasted_iota(jnp.int32, (64, 128), 0)
+                    j = lax.broadcasted_iota(jnp.int32, (64, 128), 1)
                     band = ((j - i) + (q * 128 - r - offset)) & (rows - 1)
-                    k = jnp.where(band < NEGW, -1.0 / ((1.0 + d) * (1.1 * d + 0.1)), 0.0)
+                    k = jnp.where(band < NEGW, -1.0 / (d * (1.1 * (d - 1.0) + 0.1)), 0.0)
                 k = k.astype(BF16)
-                coef[pl.ds(r, 32), cols] = k
+                coef[pl.ds(r, 64), cols] = k
                 total = total + k.astype(F32)
-            sums[pl.ds(r, 32), :] = total
+            sums[pl.ds(r, 64), :] = total
             return 0
 
-        lax.fori_loop(0, rows // 32, tile, 0)
-        acc[...] += nn(coef[...], block)
-
-    pull(far[3], None, "far", offsets[3])
+        lax.fori_loop(0, rows // 64, tile, 0)
+        acc[...] += nn(coef[:, 0:wide], block[...])
+
+    def attract(b):
+        for dx in (0, 1, 3, 2):
+            for cp in reply[b, dx]:
+                cp.wait_recv()
+            pull(table.at[dx, b * 256 : b * 256 + 256], dx, b, None)
+
+    attract(0)
+    for e in range(2):
+        to_mate[e].wait_recv()
+        for j in turns:
+            deliver(mate, 1, j, e)
+    pull(far.at[3], None, None, offsets[3])
     for s in (1, 3, 2):
         to_y[s - 1].wait_recv()
-        pull(far[s - 1], None, "far", offsets[s - 1])
-    for dx in (0, 1, 3, 2):
-        for at, cp in reply:
-            if at == dx:
-                cp.wait_recv()
-        part = xs(dx)
-        pull(table[part], part, "near", None)
+        pull(far.at[s - 1], None, None, offsets[s - 1])
+    attract(1)
 
     total = jnp.sum(sums[...], axis=1, keepdims=True)
     dcodes[...] = (scale * (total * codes[...] - acc[...])).astype(BF16)
@@ -330,6 +361,15 @@
         spread.append(cp)
     for cp in spread:
         cp.wait_recv()
+    out[...] = whole[...]
+
+    for cp in ask + [to_next] + to_mate + to_y + sum(reply.values(), []) + [core_a, core_b]:
+        cp.wait_send()
+    for cp in a1 + b1 + a2 + b2 + zs + spread:
+        cp.wait_send()
+
+
+def assemble(whole, out_first, out_second):
     for yy in range(NY):
         for ll in range(NL):
             r = yy * 16 + (ll // 2) * 8
@@ -337,11 +377,6 @@
             out_first[r : r + 8, half * 512 : half * 512 + 512] = whole[yy, ll, :, 0:512]
             out_second[r : r + 8, half * 128 : half * 128 + 128] = whole[yy, ll, :, 512:640]
 
-    for cp in ask + [to_next, to_mate] + to_y + [cp for _, cp in reply] + [core_a, core_b]:
-        cp.wait_send()
-    for cp in a1 + b1 + a2 + b2 + zs + spread:
-        cp.wait_send()
-
 
 def shards(inputs, w_first, w_second, requests, slots, counts, edge_weight, offsets):
     rows = inputs.shape[0]
@@ -349,12 +384,23 @@
     scale = 2.0 / (slots.shape[1] * math.sqrt(total_rows))
     vmem = pl.BlockSpec(memory_space=pltpu.VMEM)
     smem = pl.BlockSpec(memory_space=pltpu.SMEM)
-    return pl.pallas_call(
+    anyplace = pl.BlockSpec(memory_space=pl.ANY)
+    whole = pl.pallas_call(
         lambda *refs: step(scale, *refs),
-        out_shape=(jax.ShapeDtypeStruct((64, 1024), F32), jax.ShapeDtypeStruct((64, 256), F32)),
-        in_specs=[vmem] * 7 + [smem],
-        out_specs=(vmem, vmem),
+        out_shape=jax.ShapeDtypeStruct((NY, NL, 8, 640), F32),
+        in_specs=[anyplace] * 7 + [smem],
+        out_specs=vmem,
         scratch_shapes=[
+            pltpu.VMEM((512, 1024), BF16),
+            pltpu.VMEM((1024, 1024), BF16),
+            pltpu.VMEM((1024, 256), BF16),
+            pltpu.VMEM((16, 128), jnp.int32),
+            pltpu.VMEM((15, 512), jnp.int32),
+            pltpu.VMEM((1, 512), jnp.int32),
+            pltpu.VMEM((15, 512), jnp.int32),
+            pltpu.SemaphoreType.DMA((10,)),
+            pltpu.VMEM((2, 8, 128, 512), BF16),
+            pltpu.VMEM((512, 256), BF16),
             pltpu.VMEM((512, 1024), BF16),
             pltpu.VMEM((512, 256), F32),
             pltpu.VMEM((512, 256), BF16),
@@ -363,7 +409,7 @@
             pltpu.VMEM((8, 8, 128), jnp.int32),
             pltpu.VMEM((8, 8, 128), jnp.int32),
             pltpu.VMEM((128, 512), F32),
-            pltpu.VMEM((14, 128, 256), BF16),
+            pltpu.VMEM((2, 7, 128, 256), BF16),
             pltpu.VMEM((4, 512, 256), BF16),
             pltpu.VMEM((4, 512, 512), BF16),
             pltpu.VMEM((512, 128), F32),
@@ -394,8 +440,8 @@
             pltpu.VMEM((2, 4, 8, 640), F32),
             pltpu.VMEM((8, 8, 640), F32),
             pltpu.VMEM((4, 4, 8, 640), F32),
-            pltpu.SemaphoreType.DMA((64,)),
-            pltpu.SemaphoreType.DMA((64,)),
+            pltpu.SemaphoreType.DMA((80,)),
+            pltpu.SemaphoreType.DMA((80,)),
         ],
         compiler_params=pltpu.CompilerParams(
             collective_id=0, has_side_effects=True, vmem_limit_bytes=56 << 20
@@ -405,6 +451,13 @@
     )(
         inputs, w_first, w_second, requests, slots.T, counts.reshape(1, -1), edge_weight.T, offsets
     )
+    return pl.pallas_call(
+        assemble,
+        out_shape=(jax.ShapeDtypeStruct((64, 1024), F32), jax.ShapeDtypeStruct((64, 256), F32)),
+        in_specs=[vmem],
+        out_specs=(vmem, vmem),
+        name="assemble",
+    )(whole)
 
 
 def solution(mesh):

time: 84.1 us -> 81.5 us (0.969)
  local copies, waits for them, and re-layouts: 3.14 us -> 0 us
    unnamed x2 -> x0, local copies, waits for them, and re-layouts: 3.14 us -> none
    pallas_call x1 -> x2, Pallas kernels: 80.1 us -> 80.8 us  [the longest x1 79 us: shards(): pl.pallas_call(lambda *refs: step(scale, *refs), out_shape=jax.ShapeDtype...]
where the time goes in v2:
time: 81.5 us; the launch traced here: 81.4 us
  Pallas kernels  80.8 us (99%)
    pallas_call x1, Pallas kernels, shards(): pl.pallas_call(lambda *refs: step(scale, *refs), out_shape=jax.ShapeDtype...  79 us
    pallas_call x1, Pallas kernels, shards(): pl.pallas_call(assemble, out_shape=(jax.ShapeDtypeStruct((64, 1024), F32)...  1.71 us

profile of v2, /device:TPU:32, one launch (start us, length us, event | category | flops | bytes accessed | tf_op | source)
XLA Modules:
  0.0 81.4 jit_solution(10984477516779605270)
XLA Ops:
  0.6 79.0 %embedding_step.1.whole = f32[4,4,8,640]{3,2,1,0:T(8,128)} custom-call(bf16[512,1024]{1,0:T(8,128)(2,1)} %refs_0_.1, bf16[1024,1024]{1,0:T(8,128)(2,1)} %refs_1_.1, bf16[1024,256]{1,0:T(8,128)(2,1)} %refs_2_.1, s32[16,128]{1,0:T(8,128)} %refs_3_.1, s32[15,512]{1,0:T(8,128)} %bitcast.3, s32[1,512]{1,0:T(1,128)} %bitcast.5, s32[15,512]{1,0:T(8,128)} %bitcast.4, ...), custom_call_target="tpu_custom_call" | custom-call | flops 8999999488 | bytes 5000000 | tf_op jit(solution)/shard_map/embedding_step/pallas_call | solution.py:388
  79.7 1.7 %assemble.1 = (f32[64,1024]{1,0:T(8,128)}, f32[64,256]{1,0:T(8,128)}) custom-call(f32[4,4,8,640]{3,2,1,0:T(8,128)} %embedding_step.1.whole), custom_call_target="tpu_custom_call" | custom-call | tf_op jit(solution)/shard_map/assemble/pallas_call | solution.py:454

commit v3 on v2

v3 whole, which is shorter than its diff:
```python
import math

import jax
import jax.numpy as jnp
from jax import lax
from jax.experimental import pallas as pl
from jax.experimental.pallas import tpu as pltpu
from jax.sharding import PartitionSpec as P

MESH = pl.DeviceIdType.MESH
F32 = jnp.float32
BF16 = jnp.bfloat16
NEGW = 8
NX, NH, NC, NL, NY = 4, 2, 2, 4, 4


def nt(a, b):
    return lax.dot_general(a, b, (((1,), (1,)), ((), ())), preferred_element_type=F32)


def nn(a, b):
    return jnp.dot(a, b, preferred_element_type=F32)


def step(
    scale, inputs_hbm, w1_hbm, w2_hbm, requests_hbm, slots_hbm, counts_hbm, edges_hbm, offsets, out0, out1,
    inputs, w1, w2, requests, slots, counts, edges, in_sem, picks, sent_part, hidden, codes, sent, mate, far, reqs, asked, keys, found, table, weights, norms,
    xt, ht, sums, acc, dist, coef, dpre, dcodes, asks_f, wishes, send_sem, recv_sem, *pairs,
):
    pair0, pair1 = pairs[:19], pairs[19:]
    w = lax.axis_index("wide")
    n = lax.axis_index("narrow")
    x, h, c = w // 4, (w // 2) % 2, w % 2
    l, y = n // 4, n % 4
    rows = inputs.shape[0]
    sem_count = [0]

    loads = []

    def load(src, dst):
        cp = pltpu.make_async_copy(src, dst, in_sem.at[len(loads)])
        cp.start()
        loads.append(cp)
        return cp

    need_requests = load(requests_hbm, requests)
    need_w1 = [load(w1_hbm.at[q : q + 256], w1.at[q : q + 256]) for q in range(0, 1024, 256)]
    need_inputs = [load(inputs_hbm.at[q : q + 128], inputs.at[q : q + 128]) for q in range(0, rows, 128)]
    need_w2 = load(w2_hbm, w2)

    def device(xx, hh, cc, ll, yy):
        return (xx * 4 + hh * 2 + cc, ll * 4 + yy)

    def copy(src, dst, target):
        at = sem_count[0]
        sem_count[0] += 1
        return pltpu.make_async_remote_copy(
            src_ref=src, dst_ref=dst, send_sem=send_sem.at[at], recv_sem=recv_sem.at[at],
            device_id=target, device_id_type=MESH,
        )

    def xs(s):
        return (x + s) % NX

    def ys(s):
        return (y + s) % NY

    def ls(s):
        return (l + s) % NL

    barrier = pltpu.get_barrier_semaphore()
    plane = [(dx, dc) for dx in range(NX) for dc in range(NC) if dx or dc]
    ring = [(dl, dy) for dl in range(NL) for dy in range(NY) if dl or dy]
    peers = [device(xs(dx), h, (c + dc) % 2, l, y) for dx, dc in plane]
    peers += [device(x, h, c, ls(dl), ys(dy)) for dl, dy in ring]
    peers += [device(x, 1 - h, c, ls(dl), y) for dl in range(NL)]
    for peer in peers:
        pl.semaphore_signal(barrier, inc=1, device_id=peer, device_id_type=MESH)

    need_requests.wait()
    reqs[...] = jnp.zeros_like(reqs)
    for xx in range(NX):
        for cc in range(NC):
            for hh in range(NH):
                p = xx * 4 + hh * 2 + cc
                reqs[xx * 2 + cc, hh : hh + 1, :] = requests[p : p + 1, :]

    for cp in need_w1:
        cp.wait()
    for q in range(4):
        need_inputs[q].wait()
        for at in range(0, 1024, 256):
            pre = nn(inputs[q * 128 : q * 128 + 128, :], w1[:, at : at + 256])
            hidden[q * 128 : q * 128 + 128, at : at + 256] = jnp.maximum(pre, 0.0).astype(BF16)
        if q == 0:
            lists = [load(slots_hbm, slots), load(counts_hbm, counts), load(edges_hbm, edges)]
    need_w2.wait()
    codes[...] = nn(hidden[...], w2[...])
    sent[...] = codes[...].astype(BF16)
    sent_part[...] = sent[...] * (2.0 / 256.0)

    pl.semaphore_wait(barrier, len(peers))

    ask = []
    for dx, dc in plane:
        j = dx * 2 + dc
        cp = copy(reqs.at[xs(dx) * 2 + (c + dc) % 2], asked.at[j], device(xs(dx), h, (c + dc) % 2, l, y))
        cp.start()
        ask.append(cp)
    to_next = copy(sent, far.at[3], device(x, h, c, ls(1), y))
    to_next.start()
    to_mate = []
    for e in range(2):
        cols = slice(e * 128, e * 128 + 128)
        cp = copy(sent.at[:, cols], mate.at[:, cols], device(x, 1 - h, c, l, y))
        cp.start()
        to_mate.append(cp)
    to_y = []
    for s in (1, 2, 3):
        cp = copy(sent, far.at[s - 1], device(x, h, c, l, ys(s)))
        to_y.append(cp)
        pl.when(y + s < NY)(cp.start)

    for cp in lists:
        cp.wait()
    live = lax.broadcasted_iota(jnp.int32, slots.shape, 0) < counts[...]
    keys[...] = jnp.zeros_like(keys)
    place = ((slots[...] - x * 512) & 2047) ^ (h * 256 + c * 128)
    keys[0:15, :] = place.astype(F32)
    keys[16:31, :] = jnp.where(live, edges[...], 0).astype(F32)
    norms[...] = keys[...].T

    def weigh(at, _):
        r = pl.multiple_of(at * 16, 16)
        both = norms[pl.ds(r, 16), :]
        lane = lax.broadcasted_iota(jnp.int32, (16, 512), 1).astype(F32)
        spots = [jnp.broadcast_to(both[:, k : k + 1], (16, 512)) for k in range(15)]
        worth = [jnp.broadcast_to(both[:, 16 + k : 17 + k], (16, 512)) for k in range(15)]
        for part in range(4):
            total = jnp.zeros((16, 512), F32)
            for k in range(15):
                total = total + jnp.where(spots[k] == lane + float(part * 512), worth[k], 0.0)
            weights[part, pl.ds(r, 16), :] = total.astype(BF16)
        return 0

    for cp in ask:
        cp.wait_recv()
    asked[0] = reqs[x * 2 + c]
    for j in range(8):
        norms2 = asked[j]
        asks_f[j * 8 : j * 8 + 8, :] = norms2.astype(F32)
    wishes[...] = asks_f[...].T

    lane = lax.broadcasted_iota(jnp.int32, (128, rows), 1).astype(F32)
    reply = {}

    def deliver(block, b, j, e):
        cols = slice(0, 256) if e is None else slice(e * 128, e * 128 + 128)
        got = nn(picks[b, j], block[:, cols]).astype(BF16)
        dx, dc = j // 2, j % 2
        spot = slice(b * 256 + dc * 128, b * 256 + dc * 128 + 128)
        if j == 0:
            table[0, spot, cols] = got
        else:
            found[b, j - 1, :, cols] = got
            cp = copy(
                found.at[b, j - 1, :, cols], table.at[dx, spot, cols],
                device(xs(NX - dx), h, (c + dc) % 2, l, y),
            )
            cp.start()
            reply.setdefault((b, dx), []).append(cp)

    turns = (2, 6, 4, 3, 7, 5, 1, 0)
    def choose(b):
        for j in turns:
            which = jnp.where((h + b) % 2 == 0, wishes[:, j * 8 : j * 8 + 1], wishes[:, j * 8 + 1 : j * 8 + 2])
            picks[b, j] = jnp.where(jnp.broadcast_to(which, (128, rows)) == lane, 1.0, 0.0).astype(BF16)
            if b == 0:
                deliver(sent, 0, j, None)

    choose(0)
    lax.fori_loop(0, rows // 32, weigh, 0)
    to_next.wait_recv()
    for s in (1, 2, 3):
        cp = pltpu.make_async_remote_copy(
            src_ref=far.at[3], dst_ref=far.at[s - 1], send_sem=send_sem.at[10 + s - 1],
            recv_sem=recv_sem.at[10 + s - 1], device_id=device(x, h, c, l, ys(s)), device_id_type=MESH,
        )
        pl.when(y + s >= NY)(cp.start)
    lax.fori_loop(rows // 32, rows // 16, weigh, 0)
    choose(1)
    for g in range(8):
        xt[g * 128 : g * 128 + 128, :] = inputs[:, g * 128 : g * 128 + 128].T
        ht[g * 128 : g * 128 + 128, :] = hidden[:, g * 128 : g * 128 + 128].T

    inv = 1.0 / 256.0
    own = sent[...].astype(F32)
    norm = jnp.sum(own * own, axis=1, keepdims=True)
    norms[...] = jnp.broadcast_to(norm * inv + 1.0, norms.shape)
    sums[...] = jnp.zeros_like(sums)
    acc[...] = jnp.zeros_like(acc)
    ones = jnp.ones((8, 256), BF16)

    def squares(block):
        z = block.astype(F32)
        z = z * z
        hi = z.astype(BF16)
        lo = (z - hi.astype(F32)).astype(BF16)
        return (nt(ones, hi) + nt(ones, lo))[0:1, :] * inv

    def pull(block, dx, b, offset):
        wide = block.shape[0]
        dist[:, 0:wide] = nt(sent_part[...], block[...])
        size = squares(block[...])

        def tile(at, _):
            r = pl.multiple_of(at * 64, 64)
            mine = norms[pl.ds(r, 64), :]
            total = sums[pl.ds(r, 64), :]
            for q in range(wide // 128):
                cols = slice(q * 128, q * 128 + 128)
                d = jnp.maximum((mine + size[:, cols]) - dist[pl.ds(r, 64), cols], 1.0)
                if dx is not None:
                    at_b = slice(b * 256 + q * 128, b * 256 + q * 128 + 128)
                    k = weights[dx, pl.ds(r, 64), at_b].astype(F32) * (1.0 / d)
                else:
                    i = lax.broadcasted_iota(jnp.int32, (64, 128), 0)
                    j = lax.broadcasted_iota(jnp.int32, (64, 128), 1)
                    band = ((j - i) + (q * 128 - r - offset)) & (rows - 1)
                    k = jnp.where(band < NEGW, -1.0 / (d * (1.1 * (d - 1.0) + 0.1)), 0.0)
                k = k.astype(BF16)
                coef[pl.ds(r, 64), cols] = k
                total = total + k.astype(F32)
            sums[pl.ds(r, 64), :] = total
            return 0

        lax.fori_loop(0, rows // 64, tile, 0)
        acc[...] += nn(coef[:, 0:wide], block[...])

    def attract(b):
        for dx in (0, 1, 3, 2):
            for cp in reply[b, dx]:
                cp.wait_recv()
            pull(table.at[dx, b * 256 : b * 256 + 256], dx, b, None)

    attract(0)
    for e in range(2):
        to_mate[e].wait_recv()
        for j in turns:
            deliver(mate, 1, j, e)
    pull(far.at[3], None, None, offsets[3])
    for s in (1, 3, 2):
        to_y[s - 1].wait_recv()
        pull(far.at[s - 1], None, None, offsets[s - 1])
    attract(1)

    total = jnp.sum(sums[...], axis=1, keepdims=True)
    dcodes[...] = (scale * (total * codes[...] - acc[...])).astype(BF16)

    core = device(x, h, 1 - c, l, y)

    def backward(g, first, width):
        for at in range(first, first + width, 128):
            back = nt(dcodes[...], w2[at : at + 128, :])
            dpre[:, at : at + 128] = jnp.where(hidden[:, at : at + 128] > 0, back, 0.0).astype(BF16)
        g[...] = nn(xt[...], dpre[:, first : first + width])

    def part_rows(xx, hh, cc, yy):
        return pl.ds(pl.multiple_of(xx * 256 + hh * 128 + cc * 64 + yy * 16, 16), 16)

    each = [(xx, hh, yy) for xx in range(NX) for hh in range(NH) for yy in range(NY)]
    sends = []

    def go(src, dst, target):
        cp = copy(src, dst, target)
        cp.start()
        sends.append(cp)
        return cp

    def spot(kind, xx, hh, yy):
        return (xx, hh, yy) if kind == "a" else (yy, hh, xx)

    class Chunk:
        def __init__(self, kind, g, c_out, c_in, p_out, p_in, f, q_out, q_in):
            self.kind, self.g, self.c_out, self.c_in, self.p_out, self.p_in = kind, g, c_out, c_in, p_out, p_in
            self.f, self.q_out, self.q_in = f, q_out, q_in

        def near(self, s):
            return (xs(s), device(xs(s), h, c, l, y)) if self.kind == "a" else (ys(s), device(x, h, c, l, ys(s)))

        def beyond(self, s):
            return (ys(s), device(x, h, c, l, ys(s))) if self.kind == "a" else (xs(s), device(xs(s), h, c, l, y))

        def to_core(self):
            for xx, hh, yy in each:
                self.c_out[spot(self.kind, xx, hh, yy)] = self.g[part_rows(xx, hh, 1 - c, yy), :].astype(BF16)
            self.core = go(self.c_out, self.c_in, core)

        def first(self):
            self.core.wait_recv()
            for xx, hh, yy in each:
                at = spot(self.kind, xx, hh, yy)
                self.p_out[at] = (self.g[part_rows(xx, hh, c, yy), :] + self.c_in[at].astype(F32)).astype(BF16)
            self.one = []
            for s in (2, 1, 3):
                at, target = self.near(s)
                self.one.append(go(self.p_out.at[at], self.p_in.at[s - 1], target))
            mine = x if self.kind == "a" else y
            for far_at in range(4):
                for hh in range(NH):
                    rows_at = part_rows(x, hh, c, far_at) if self.kind == "a" else part_rows(far_at, hh, c, y)
                    self.f[hh, far_at] = self.g[rows_at, :] + self.c_in[mine, hh, far_at].astype(F32)

        def second(self):
            for cp in self.one:
                cp.wait_recv()
            for hh in range(NH):
                for far_at in range(4):
                    got = [self.p_in[s, hh, far_at].astype(F32) for s in range(3)]
                    self.f[hh, far_at] += got[0] + got[1] + got[2]
                    self.q_out[far_at, hh] = self.f[hh, far_at].astype(BF16)
            self.two = []
            for s in (2, 1, 3):
                at, target = self.beyond(s)
                self.two.append(go(self.q_out.at[at], self.q_in.at[s - 1], target))

        def result(self, hh):
            mine = y if self.kind == "a" else x
            got = [self.q_in[s, hh].astype(F32) for s in range(3)]
            return self.f[hh, mine] + got[0] + got[1] + got[2]

    class Pair:
        def __init__(self, a, b, zs_out, zs_in, whole):
            self.a, self.b, self.zs_out, self.zs_in, self.whole = a, b, zs_out, zs_in, whole

        def over_z(self):
            for cp in self.a.two + self.b.two:
                cp.wait_recv()
            for hh in range(NH):
                for half, chunk in enumerate((self.a, self.b)):
                    total = chunk.result(hh)
                    self.zs_out[hh, half] = total[0:8, :]
                    self.zs_out[hh, 2 + half] = total[8:16, :]
            self.zs = []
            for dh, dl in ((1, 0), (1, 2), (1, 1), (1, 3), (0, 2), (0, 1), (0, 3)):
                hh = (h + dh) % 2
                self.zs.append(
                    go(self.zs_out.at[hh, ls(dl)], self.zs_in.at[dh * 4 + dl], device(x, hh, c, ls(dl), y))
                )

        def spread(self):
            total = self.zs_out[h, l]
            for cp in self.zs:
                cp.wait_recv()
            for k in range(1, 8):
                total = total + self.zs_in[k]
            self.whole[y, l] = total
            self.last = [
                go(self.whole.at[y, l], self.whole.at[y, l], device(x, h, c, ls(dl), ys(dy)))
                for dl, dy in ring
            ]

    a0, b0 = Chunk("a", *pair0[0:8]), Chunk("b", *pair0[8:16])
    a1, b1 = Chunk("a", *pair1[0:8]), Chunk("b", *pair1[8:16])
    p0, p1 = Pair(a0, b0, *pair0[16:19]), Pair(a1, b1, *pair1[16:19])
    backward(b0.g, 0, 384)
    b0.to_core()
    backward(a0.g, 384, 384)
    a0.to_core()
    b0.first()
    a0.first()
    a1.g[...] = nn(ht[...], dcodes[...])
    a1.to_core()
    backward(b1.g, 768, 256)
    b1.to_core()
    a1.first()
    b1.first()
    b0.second()
    a0.second()
    a1.second()
    b1.second()
    p0.over_z()
    p1.over_z()
    p0.spread()
    p1.spread()
    for cp in p0.last:
        cp.wait_recv()
    out0[...] = p0.whole[...]
    for cp in p1.last:
        cp.wait_recv()
    out1[...] = p1.whole[...]

    for cp in ask + [to_next] + to_mate + to_y + sum(reply.values(), []) + sends:
        cp.wait_send()


def pair_scratch(width):
    chunk = [
        pltpu.VMEM((1024, width), F32),
        pltpu.VMEM((4, 2, 4, 16, width), BF16),
        pltpu.VMEM((4, 2, 4, 16, width), BF16),
        pltpu.VMEM((4, 2, 4, 16, width), BF16),
        pltpu.VMEM((3, 2, 4, 16, width), BF16),
        pltpu.VMEM((2, 4, 16, width), F32),
        pltpu.VMEM((4, 2, 16, width), BF16),
        pltpu.VMEM((3, 2, 16, width), BF16),
    ]
    shared = [
        pltpu.VMEM((2, 4, 8, width), F32),
        pltpu.VMEM((8, 8, width), F32),
        pltpu.VMEM((4, 4, 8, width), F32),
    ]
    return chunk + chunk + shared


def assemble(whole0, whole1, out_first, out_second):
    for yy in range(NY):
        for ll in range(NL):
            at = slice(yy * 16 + (ll // 2) * 8, yy * 16 + (ll // 2) * 8 + 8)
            if ll % 2 == 0:
                out_first[at, 384:768] = whole0[yy, ll]
                out_second[at, :] = whole1[yy, ll]
            else:
                out_first[at, 0:384] = whole0[yy, ll]
                out_first[at, 768:1024] = whole1[yy, ll]


def shards(inputs, w_first, w_second, requests, slots, counts, edge_weight, offsets):
    rows = inputs.shape[0]
    total_rows = rows * lax.axis_size("wide") * lax.axis_size("narrow")
    scale = 2.0 / (slots.shape[1] * math.sqrt(total_rows))
    vmem = pl.BlockSpec(memory_space=pltpu.VMEM)
    smem = pl.BlockSpec(memory_space=pltpu.SMEM)
    anyplace = pl.BlockSpec(memory_space=pl.ANY)
    whole0, whole1 = pl.pallas_call(
        lambda *refs: step(scale, *refs),
        out_shape=(
            jax.ShapeDtypeStruct((NY, NL, 8, 384), F32),
            jax.ShapeDtypeStruct((NY, NL, 8, 256), F32),
        ),
        in_specs=[anyplace] * 7 + [smem],
        out_specs=(vmem, vmem),
        scratch_shapes=[
            pltpu.VMEM((512, 1024), BF16),
            pltpu.VMEM((1024, 1024), BF16),
            pltpu.VMEM((1024, 256), BF16),
            pltpu.VMEM((16, 128), jnp.int32),
            pltpu.VMEM((15, 512), jnp.int32),
            pltpu.VMEM((1, 512), jnp.int32),
            pltpu.VMEM((15, 512), jnp.int32),
            pltpu.SemaphoreType.DMA((16,)),
            pltpu.VMEM((2, 8, 128, 512), BF16),
            pltpu.VMEM((512, 256), BF16),
            pltpu.VMEM((512, 1024), BF16),
            pltpu.VMEM((512, 256), F32),
            pltpu.VMEM((512, 256), BF16),
            pltpu.VMEM((512, 256), BF16),
            pltpu.VMEM((4, 512, 256), BF16),
            pltpu.VMEM((8, 8, 128), jnp.int32),
            pltpu.VMEM((8, 8, 128), jnp.int32),
            pltpu.VMEM((128, 512), F32),
            pltpu.VMEM((2, 7, 128, 256), BF16),
            pltpu.VMEM((4, 512, 256), BF16),
            pltpu.VMEM((4, 512, 512), BF16),
            pltpu.VMEM((512, 128), F32),
            pltpu.VMEM((1024, 512), BF16),
            pltpu.VMEM((1024, 512), BF16),
            pltpu.VMEM((512, 128), F32),
            pltpu.VMEM((512, 256), F32),
            pltpu.VMEM((512, 512), F32),
            pltpu.VMEM((512, 512), BF16),
            pltpu.VMEM((512, 1024), BF16),
            pltpu.VMEM((512, 256), BF16),
            pltpu.VMEM((128, 128), F32),
            pltpu.VMEM((128, 128), F32),
            pltpu.SemaphoreType.DMA((128,)),
            pltpu.SemaphoreType.DMA((128,)),
        ]
        + pair_scratch(384)
        + pair_scratch(256),
        compiler_params=pltpu.CompilerParams(
            collective_id=0, has_side_effects=True, vmem_limit_bytes=56 << 20
        ),
        cost_estimate=pl.CostEstimate(flops=9_000_000_000, bytes_accessed=5_000_000, transcendentals=0),
        name="embedding_step",
    )(
        inputs, w_first, w_second, requests, slots.T, counts.reshape(1, -1), edge_weight.T, offsets
    )
    return pl.pallas_call(
        assemble,
        out_shape=(jax.ShapeDtypeStruct((64, 1024), F32), jax.ShapeDtypeStruct((64, 256), F32)),
        in_specs=[vmem, vmem],
        out_specs=(vmem, vmem),
        name="assemble",
    )(whole0, whole1)


def solution(mesh):
    return jax.shard_map(
        shards,
        mesh=mesh,
        in_specs=(
            P(("wide", "narrow"), None),
            P(),
            P(),
            P(("wide", "narrow"), None),
            P(("wide", "narrow"), None),
            P(("wide", "narrow")),
            P(("wide", "narrow"), None),
            P(),
        ),
        out_specs=(P("wide", None), P("wide", None)),
        check_vma=False,
    )
```

time: 81.5 us -> 80.5 us (0.988)
  Pallas kernels: 80.8 us -> 79.4 us
    pallas_call x1, Pallas kernels: 79 us -> 77.6 us  [shards(): pl.pallas_call(lambda *refs: step(scale, *refs), out_shape=(jax.ShapeDtyp...]
where the time goes in v3:
time: 80.5 us; the launch traced here: 80 us
  Pallas kernels  79.4 us (99%)
    pallas_call x1, Pallas kernels, shards(): pl.pallas_call(lambda *refs: step(scale, *refs), out_shape=(jax.ShapeDtyp...  77.6 us
    pallas_call x1, Pallas kernels, shards(): pl.pallas_call(assemble, out_shape=(jax.ShapeDtypeStruct((64, 1024), F32)...  1.75 us

profile of v3, /device:TPU:32, one launch (start us, length us, event | category | flops | bytes accessed | tf_op | source)
XLA Modules:
  0.0 80.0 jit_solution(13631828412423802169)
XLA Ops:
  0.6 77.6 %embedding_step.1 = (f32[4,4,8,384]{3,2,1,0:T(8,128)}, f32[4,4,8,256]{3,2,1,0:T(8,128)}) custom-call(bf16[512,1024]{1,0:T(8,128)(2,1)} %refs_0_.1, bf16[1024,1024]{1,0:T(8,128)(2,1)} %refs_1_.1, bf16[1024,256]{1,0:T(8,128)(2,1)} %refs_2_.1, s32[16,128]{1,0:T(8,128)} %refs_3_.1, s32[15,512]{1,0:T(8,128)} %bitcast.3, s32[1,512]{1,0:T(1,128)} %bitcast.5, ...), custom_call_target="tpu_custom_call" | custom-call | flops 8999999488 | bytes 5000000 | tf_op jit(solution)/shard_map/embedding_step/pallas_call | solution.py:435
  78.3 1.7 %assemble.1 = (f32[64,1024]{1,0:T(8,128)}, f32[64,256]{1,0:T(8,128)}) custom-call(f32[4,4,8,384]{3,2,1,0:T(8,128)} %get-tuple-element.4.whole0, f32[4,4,8,256]{3,2,1,0:T(8,128)} %get-tuple-element.5.whole1), custom_call_target="tpu_custom_call" | custom-call | tf_op jit(solution)/shard_map/assemble/pallas_call | solution.py:489

commit v4 on v3

--- a/solution.py
+++ b/solution.py
@@ -43,6 +43,7 @@
         loads.append(cp)
         return cp
 
+    lists = [load(slots_hbm, slots), load(counts_hbm, counts), load(edges_hbm, edges)]
     need_requests = load(requests_hbm, requests)
     need_w1 = [load(w1_hbm.at[q : q + 256], w1.at[q : q + 256]) for q in range(0, 1024, 256)]
     need_inputs = [load(inputs_hbm.at[q : q + 128], inputs.at[q : q + 128]) for q in range(0, rows, 128)]
@@ -85,6 +86,32 @@
                 p = xx * 4 + hh * 2 + cc
                 reqs[xx * 2 + cc, hh : hh + 1, :] = requests[p : p + 1, :]
 
+    for cp in lists:
+        cp.wait()
+    live = lax.broadcasted_iota(jnp.int32, slots.shape, 0) < counts[...]
+    place = ((slots[...] - x * 512) & 2047) ^ (h * 256 + c * 128)
+    worth = jnp.where(live, edges[...], 0) << (((place >> 7) & 3) * 8)
+    keys[...] = jnp.zeros_like(keys)
+    keys[0:15, :] = (((place >> 9) << 7) | (place & 127)).astype(F32)
+    keys[16:31, :] = worth.astype(F32)
+    norms[...] = keys[...].T
+
+    def weigh(at, _):
+        r = pl.multiple_of(at * 16, 16)
+        both = norms[pl.ds(r, 16), :].astype(jnp.int32)
+        lane = lax.broadcasted_iota(jnp.int32, (16, 128), 1)
+        total = [jnp.zeros((16, 128), jnp.int32) for _ in range(4)]
+        for k in range(15):
+            spot = jnp.broadcast_to(both[:, k : k + 1], (16, 128))
+            value = jnp.broadcast_to(both[:, 16 + k : 17 + k], (16, 128))
+            for part in range(4):
+                total[part] = total[part] + jnp.where(spot == lane + part * 128, value, 0)
+        for part in range(4):
+            weights[part, pl.ds(r, 16), :] = total[part]
+        return 0
+
+    lax.fori_loop(0, rows // 32, weigh, 0)
+
     for cp in need_w1:
         cp.wait()
     for q in range(4):
@@ -92,8 +119,6 @@
         for at in range(0, 1024, 256):
             pre = nn(inputs[q * 128 : q * 128 + 128, :], w1[:, at : at + 256])
             hidden[q * 128 : q * 128 + 128, at : at + 256] = jnp.maximum(pre, 0.0).astype(BF16)
-        if q == 0:
-            lists = [load(slots_hbm, slots), load(counts_hbm, counts), load(edges_hbm, edges)]
     need_w2.wait()
     codes[...] = nn(hidden[...], w2[...])
     sent[...] = codes[...].astype(BF16)
@@ -121,28 +146,8 @@
         to_y.append(cp)
         pl.when(y + s < NY)(cp.start)
 
-    for cp in lists:
-        cp.wait()
-    live = lax.broadcasted_iota(jnp.int32, slots.shape, 0) < counts[...]
-    keys[...] = jnp.zeros_like(keys)
-    place = ((slots[...] - x * 512) & 2047) ^ (h * 256 + c * 128)
-    keys[0:15, :] = place.astype(F32)
-    keys[16:31, :] = jnp.where(live, edges[...], 0).astype(F32)
-    norms[...] = keys[...].T
-
-    def weigh(at, _):
-        r = pl.multiple_of(at * 16, 16)
-        both = norms[pl.ds(r, 16), :]
-        lane = lax.broadcasted_iota(jnp.int32, (16, 512), 1).astype(F32)
-        spots = [jnp.broadcast_to(both[:, k : k + 1], (16, 512)) for k in range(15)]
-        worth = [jnp.broadcast_to(both[:, 16 + k : 17 + k], (16, 512)) for k in range(15)]
-        for part in range(4):
-            total = jnp.zeros((16, 512), F32)
-            for k in range(15):
-                total = total + jnp.where(spots[k] == lane + float(part * 512), worth[k], 0.0)
-            weights[part, pl.ds(r, 16), :] = total.astype(BF16)
-        return 0
-
+    for g in range(8):
+        xt[g * 128 : g * 128 + 128, :] = inputs[:, g * 128 : g * 128 + 128].T
     for cp in ask:
         cp.wait_recv()
     asked[0] = reqs[x * 2 + c]
@@ -179,7 +184,7 @@
                 deliver(sent, 0, j, None)
 
     choose(0)
-    lax.fori_loop(0, rows // 32, weigh, 0)
+    lax.fori_loop(rows // 32, rows // 16, weigh, 0)
     to_next.wait_recv()
     for s in (1, 2, 3):
         cp = pltpu.make_async_remote_copy(
@@ -187,10 +192,8 @@
             recv_sem=recv_sem.at[10 + s - 1], device_id=device(x, h, c, l, ys(s)), device_id_type=MESH,
         )
         pl.when(y + s >= NY)(cp.start)
-    lax.fori_loop(rows // 32, rows // 16, weigh, 0)
     choose(1)
     for g in range(8):
-        xt[g * 128 : g * 128 + 128, :] = inputs[:, g * 128 : g * 128 + 128].T
         ht[g * 128 : g * 128 + 128, :] = hidden[:, g * 128 : g * 128 + 128].T
 
     inv = 1.0 / 256.0
@@ -221,8 +224,8 @@
                 cols = slice(q * 128, q * 128 + 128)
                 d = jnp.maximum((mine + size[:, cols]) - dist[pl.ds(r, 64), cols], 1.0)
                 if dx is not None:
-                    at_b = slice(b * 256 + q * 128, b * 256 + q * 128 + 128)
-                    k = weights[dx, pl.ds(r, 64), at_b].astype(F32) * (1.0 / d)
+                    count = (weights[dx, pl.ds(r, 64), :] >> (8 * (b * 2 + q))) & 255
+                    k = count.astype(F32) * (1.0 / d)
                 else:
                     i = lax.broadcasted_iota(jnp.int32, (64, 128), 0)
                     j = lax.broadcasted_iota(jnp.int32, (64, 128), 1)
@@ -355,10 +358,22 @@
             for k in range(1, 8):
                 total = total + self.zs_in[k]
             self.whole[y, l] = total
-            self.last = [
-                go(self.whole.at[y, l], self.whole.at[y, l], device(x, h, c, ls(dl), ys(dy)))
-                for dl, dy in ring
-            ]
+            self.along = {}
+            self.last = []
+            for dl in (2, 1, 3):
+                piece = self.whole.at[y, l]
+                self.along[dl] = go(piece, piece, device(x, h, c, ls(dl), y))
+            self.pass_on(l)
+
+        def pass_on(self, ll):
+            for s in (2, 1, 3):
+                piece = self.whole.at[y, ll]
+                self.last.append(go(piece, piece, device(x, h, c, l, ys(s))))
+
+        def relay(self):
+            for dl in (1, 3, 2):
+                self.along[dl].wait_recv()
+                self.pass_on(ls(NL - dl))
 
     a0, b0 = Chunk("a", *pair0[0:8]), Chunk("b", *pair0[8:16])
     a1, b1 = Chunk("a", *pair1[0:8]), Chunk("b", *pair1[8:16])
@@ -383,6 +398,8 @@
     p1.over_z()
     p0.spread()
     p1.spread()
+    p0.relay()
+    p1.relay()
     for cp in p0.last:
         cp.wait_recv()
     out0[...] = p0.whole[...]
@@ -461,7 +478,7 @@
             pltpu.VMEM((128, 512), F32),
             pltpu.VMEM((2, 7, 128, 256), BF16),
             pltpu.VMEM((4, 512, 256), BF16),
-            pltpu.VMEM((4, 512, 512), BF16),
+            pltpu.VMEM((4, 512, 128), jnp.int32),
             pltpu.VMEM((512, 128), F32),
             pltpu.VMEM((1024, 512), BF16),
             pltpu.VMEM((1024, 512), BF16),

time: 80.5 us -> 79.6 us (0.989)
  no operation moved by 1% of the time
where the time goes in v4:
time: 79.6 us; the launch traced here: 79.4 us
  Pallas kernels  78.8 us (99%)
    pallas_call x1, Pallas kernels, shards(): pl.pallas_call(lambda *refs: step(scale, *refs), out_shape=(jax.ShapeDtyp...  77.1 us
    pallas_call x1, Pallas kernels, shards(): pl.pallas_call(assemble, out_shape=(jax.ShapeDtypeStruct((64, 1024), F32)...  1.75 us

profile of v4, /device:TPU:32, one launch (start us, length us, event | category | flops | bytes accessed | tf_op | source)
XLA Modules:
  0.0 79.4 jit_solution(11946793642481542857)
XLA Ops:
  0.6 77.1 %embedding_step.1 = (f32[4,4,8,384]{3,2,1,0:T(8,128)}, f32[4,4,8,256]{3,2,1,0:T(8,128)}) custom-call(bf16[512,1024]{1,0:T(8,128)(2,1)} %refs_0_.1, bf16[1024,1024]{1,0:T(8,128)(2,1)} %refs_1_.1, bf16[1024,256]{1,0:T(8,128)(2,1)} %refs_2_.1, s32[16,128]{1,0:T(8,128)} %refs_3_.1, s32[15,512]{1,0:T(8,128)} %bitcast.3, s32[1,512]{1,0:T(1,128)} %bitcast.5, ...), custom_call_target="tpu_custom_call" | custom-call | flops 8999999488 | bytes 5000000 | tf_op jit(solution)/shard_map/embedding_step/pallas_call | solution.py:452
  77.7 1.7 %assemble.1 = (f32[64,1024]{1,0:T(8,128)}, f32[64,256]{1,0:T(8,128)}) custom-call(f32[4,4,8,384]{3,2,1,0:T(8,128)} %get-tuple-element.4.whole0, f32[4,4,8,256]{3,2,1,0:T(8,128)} %get-tuple-element.5.whole1), custom_call_target="tpu_custom_call" | custom-call | tf_op jit(solution)/shard_map/assemble/pallas_call | solution.py:506

commit v5 on v4

--- a/solution.py
+++ b/solution.py
@@ -46,8 +46,9 @@
     lists = [load(slots_hbm, slots), load(counts_hbm, counts), load(edges_hbm, edges)]
     need_requests = load(requests_hbm, requests)
     need_w1 = [load(w1_hbm.at[q : q + 256], w1.at[q : q + 256]) for q in range(0, 1024, 256)]
-    need_inputs = [load(inputs_hbm.at[q : q + 128], inputs.at[q : q + 128]) for q in range(0, rows, 128)]
+    need_inputs = [load(inputs_hbm.at[q : q + 128], inputs.at[q : q + 128]) for q in (0, 128)]
     need_w2 = load(w2_hbm, w2)
+    need_inputs += [load(inputs_hbm.at[q : q + 128], inputs.at[q : q + 128]) for q in (256, 384)]
 
     def device(xx, hh, cc, ll, yy):
         return (xx * 4 + hh * 2 + cc, ll * 4 + yy)
@@ -59,6 +60,12 @@
             src_ref=src, dst_ref=dst, send_sem=send_sem.at[at], recv_sem=recv_sem.at[at],
             device_id=target, device_id_type=MESH,
         )
+
+    gone = []
+
+    def left(cp):
+        cp.wait_send()
+        gone.append(id(cp))
 
     def xs(s):
         return (x + s) % NX
@@ -110,20 +117,25 @@
             weights[part, pl.ds(r, 16), :] = total[part]
         return 0
 
-    lax.fori_loop(0, rows // 32, weigh, 0)
+    lax.fori_loop(0, 8, weigh, 0)
 
     for cp in need_w1:
         cp.wait()
-    for q in range(4):
-        need_inputs[q].wait()
-        for at in range(0, 1024, 256):
-            pre = nn(inputs[q * 128 : q * 128 + 128, :], w1[:, at : at + 256])
-            hidden[q * 128 : q * 128 + 128, at : at + 256] = jnp.maximum(pre, 0.0).astype(BF16)
-    need_w2.wait()
-    codes[...] = nn(hidden[...], w2[...])
-    sent[...] = codes[...].astype(BF16)
-    sent_part[...] = sent[...] * (2.0 / 256.0)
-
+
+    def forward(half):
+        for q in (2 * half, 2 * half + 1):
+            need_inputs[q].wait()
+            for at in range(0, 1024, 256):
+                pre = nn(inputs[q * 128 : q * 128 + 128, :], w1[:, at : at + 256])
+                hidden[q * 128 : q * 128 + 128, at : at + 256] = jnp.maximum(pre, 0.0).astype(BF16)
+        if half == 0:
+            need_w2.wait()
+        some = slice(half * 256, half * 256 + 256)
+        codes[some, :] = nn(hidden[some, :], w2[...])
+        sent[some, :] = codes[some, :].astype(BF16)
+        sent_part[some, :] = sent[some, :] * (2.0 / 256.0)
+
+    forward(0)
     pl.semaphore_wait(barrier, len(peers))
 
     ask = []
@@ -132,14 +144,16 @@
         cp = copy(reqs.at[xs(dx) * 2 + (c + dc) % 2], asked.at[j], device(xs(dx), h, (c + dc) % 2, l, y))
         cp.start()
         ask.append(cp)
-    to_next = copy(sent, far.at[3], device(x, h, c, ls(1), y))
-    to_next.start()
+    to_next = [
+        copy(sent.at[at : at + 256], far.at[3, at : at + 256], device(x, h, c, ls(1), y)) for at in (0, 256)
+    ]
+    to_next[0].start()
+    forward(1)
+    to_next[1].start()
     to_mate = []
     for e in range(2):
         cols = slice(e * 128, e * 128 + 128)
-        cp = copy(sent.at[:, cols], mate.at[:, cols], device(x, 1 - h, c, l, y))
-        cp.start()
-        to_mate.append(cp)
+        to_mate.append(copy(sent.at[:, cols], mate.at[:, cols], device(x, 1 - h, c, l, y)))
     to_y = []
     for s in (1, 2, 3):
         cp = copy(sent, far.at[s - 1], device(x, h, c, l, ys(s)))
@@ -184,14 +198,20 @@
                 deliver(sent, 0, j, None)
 
     choose(0)
-    lax.fori_loop(rows // 32, rows // 16, weigh, 0)
-    to_next.wait_recv()
+    for cp in to_next:
+        left(cp)
+    to_mate[0].start()
+    for cp in to_next:
+        cp.wait_recv()
     for s in (1, 2, 3):
         cp = pltpu.make_async_remote_copy(
-            src_ref=far.at[3], dst_ref=far.at[s - 1], send_sem=send_sem.at[10 + s - 1],
-            recv_sem=recv_sem.at[10 + s - 1], device_id=device(x, h, c, l, ys(s)), device_id_type=MESH,
+            src_ref=far.at[3], dst_ref=far.at[s - 1], send_sem=send_sem.at[11 + s - 1],
+            recv_sem=recv_sem.at[11 + s - 1], device_id=device(x, h, c, l, ys(s)), device_id_type=MESH,
         )
         pl.when(y + s >= NY)(cp.start)
+    lax.fori_loop(8, rows // 16, weigh, 0)
+    left(to_mate[0])
+    to_mate[1].start()
     choose(1)
     for g in range(8):
         ht[g * 128 : g * 128 + 128, :] = hidden[:, g * 128 : g * 128 + 128].T
@@ -246,12 +266,15 @@
                 cp.wait_recv()
             pull(table.at[dx, b * 256 : b * 256 + 256], dx, b, None)
 
-    attract(0)
-    for e in range(2):
+    def serve_mate(e):
         to_mate[e].wait_recv()
         for j in turns:
             deliver(mate, 1, j, e)
+
+    attract(0)
+    serve_mate(0)
     pull(far.at[3], None, None, offsets[3])
+    serve_mate(1)
     for s in (1, 3, 2):
         to_y[s - 1].wait_recv()
         pull(far.at[s - 1], None, None, offsets[s - 1])
@@ -388,6 +411,8 @@
     a1.to_core()
     backward(b1.g, 768, 256)
     b1.to_core()
+    for cp in a0.one + b0.one:
+        left(cp)
     a1.first()
     b1.first()
     b0.second()
@@ -407,8 +432,9 @@
         cp.wait_recv()
     out1[...] = p1.whole[...]
 
-    for cp in ask + [to_next] + to_mate + to_y + sum(reply.values(), []) + sends:
-        cp.wait_send()
+    for cp in ask + to_next + to_mate + to_y + sum(reply.values(), []) + sends:
+        if id(cp) not in gone:
+            cp.wait_send()
 
 
 def pair_scratch(width):

time: 79.6 us -> 76.7 us (0.964); the launches traced: 79.4 us -> 75.6 us
  Pallas kernels: 78.8 us -> 75 us
    pallas_call x1, Pallas kernels: 77.1 us -> 73.2 us  [shards(): pl.pallas_call(lambda *refs: step(scale, *refs), out_shape=(jax.ShapeDtyp...]
where the time goes in v5:
time: 76.7 us; the launch traced here: 75.6 us
  Pallas kernels  75 us (98%)
    pallas_call x1, Pallas kernels, shards(): pl.pallas_call(lambda *refs: step(scale, *refs), out_shape=(jax.ShapeDtyp...  73.2 us
    pallas_call x1, Pallas kernels, shards(): pl.pallas_call(assemble, out_shape=(jax.ShapeDtypeStruct((64, 1024), F32)...  1.75 us

profile of v5, /device:TPU:32, one launch (start us, length us, event | category | flops | bytes accessed | tf_op | source)
XLA Modules:
  0.0 75.6 jit_solution(16496978454671266585)
XLA Ops:
  0.6 73.2 %embedding_step.1 = (f32[4,4,8,384]{3,2,1,0:T(8,128)}, f32[4,4,8,256]{3,2,1,0:T(8,128)}) custom-call(bf16[512,1024]{1,0:T(8,128)(2,1)} %refs_0_.1, bf16[1024,1024]{1,0:T(8,128)(2,1)} %refs_1_.1, bf16[1024,256]{1,0:T(8,128)(2,1)} %refs_2_.1, s32[16,128]{1,0:T(8,128)} %refs_3_.1, s32[15,512]{1,0:T(8,128)} %bitcast.3, s32[1,512]{1,0:T(1,128)} %bitcast.5, ...), custom_call_target="tpu_custom_call" | custom-call | flops 8999999488 | bytes 5000000 | tf_op jit(solution)/shard_map/embedding_step/pallas_call | solution.py:478
  73.9 1.7 %assemble.1 = (f32[64,1024]{1,0:T(8,128)}, f32[64,256]{1,0:T(8,128)}) custom-call(f32[4,4,8,384]{3,2,1,0:T(8,128)} %get-tuple-element.4.whole0, f32[4,4,8,256]{3,2,1,0:T(8,128)} %get-tuple-element.5.whole1), custom_call_target="tpu_custom_call" | custom-call | tf_op jit(solution)/shard_map/assemble/pallas_call | solution.py:532

commit v6 on v5

--- a/solution.py
+++ b/solution.py
@@ -27,7 +27,7 @@
     inputs, w1, w2, requests, slots, counts, edges, in_sem, picks, sent_part, hidden, codes, sent, mate, far, reqs, asked, keys, found, table, weights, norms,
     xt, ht, sums, acc, dist, coef, dpre, dcodes, asks_f, wishes, send_sem, recv_sem, *pairs,
 ):
-    pair0, pair1 = pairs[:19], pairs[19:]
+    pair0, pair1 = pairs[:20], pairs[20:]
     w = lax.axis_index("wide")
     n = lax.axis_index("narrow")
     x, h, c = w // 4, (w // 2) % 2, w % 2
@@ -154,6 +154,7 @@
     for e in range(2):
         cols = slice(e * 128, e * 128 + 128)
         to_mate.append(copy(sent.at[:, cols], mate.at[:, cols], device(x, 1 - h, c, l, y)))
+    to_mate[0].start()
     to_y = []
     for s in (1, 2, 3):
         cp = copy(sent, far.at[s - 1], device(x, h, c, l, ys(s)))
@@ -200,7 +201,7 @@
     choose(0)
     for cp in to_next:
         left(cp)
-    to_mate[0].start()
+    to_mate[1].start()
     for cp in to_next:
         cp.wait_recv()
     for s in (1, 2, 3):
@@ -210,8 +211,6 @@
         )
         pl.when(y + s >= NY)(cp.start)
     lax.fori_loop(8, rows // 16, weigh, 0)
-    left(to_mate[0])
-    to_mate[1].start()
     choose(1)
     for g in range(8):
         ht[g * 128 : g * 128 + 128, :] = hidden[:, g * 128 : g * 128 + 128].T
@@ -356,8 +355,9 @@
             return self.f[hh, mine] + got[0] + got[1] + got[2]
 
     class Pair:
-        def __init__(self, a, b, zs_out, zs_in, whole):
-            self.a, self.b, self.zs_out, self.zs_in, self.whole = a, b, zs_out, zs_in, whole
+        def __init__(self, a, b, by_columns, zs_own, zs_out, zs_in, whole):
+            self.a, self.b, self.by_columns, self.zs_own = a, b, by_columns, zs_own
+            self.zs_out, self.zs_in, self.whole = zs_out, zs_in, whole
 
         def over_z(self):
             for cp in self.a.two + self.b.two:
@@ -365,8 +365,13 @@
             for hh in range(NH):
                 for half, chunk in enumerate((self.a, self.b)):
                     total = chunk.result(hh)
-                    self.zs_out[hh, half] = total[0:8, :]
-                    self.zs_out[hh, 2 + half] = total[8:16, :]
+                    if self.by_columns:
+                        pieces = ((2 * half, total[:, 0:256]), (2 * half + 1, total[:, 256:512]))
+                    else:
+                        pieces = ((half, total[0:8, :]), (2 + half, total[8:16, :]))
+                    for ll, piece in pieces:
+                        self.zs_own[hh, ll] = piece
+                        self.zs_out[hh, ll] = piece.astype(self.zs_out.dtype)
             self.zs = []
             for dh, dl in ((1, 0), (1, 2), (1, 1), (1, 3), (0, 2), (0, 1), (0, 3)):
                 hh = (h + dh) % 2
@@ -375,11 +380,11 @@
                 )
 
         def spread(self):
-            total = self.zs_out[h, l]
+            total = self.zs_own[h, l]
             for cp in self.zs:
                 cp.wait_recv()
             for k in range(1, 8):
-                total = total + self.zs_in[k]
+                total = total + self.zs_in[k].astype(F32)
             self.whole[y, l] = total
             self.along = {}
             self.last = []
@@ -400,16 +405,16 @@
 
     a0, b0 = Chunk("a", *pair0[0:8]), Chunk("b", *pair0[8:16])
     a1, b1 = Chunk("a", *pair1[0:8]), Chunk("b", *pair1[8:16])
-    p0, p1 = Pair(a0, b0, *pair0[16:19]), Pair(a1, b1, *pair1[16:19])
-    backward(b0.g, 0, 384)
+    p0, p1 = Pair(a0, b0, True, *pair0[16:20]), Pair(a1, b1, False, *pair1[16:20])
+    backward(b0.g, 0, 512)
     b0.to_core()
-    backward(a0.g, 384, 384)
+    backward(a0.g, 512, 512)
     a0.to_core()
     b0.first()
     a0.first()
-    a1.g[...] = nn(ht[...], dcodes[...])
+    a1.g[...] = nn(ht[...], dcodes[:, 0:128])
     a1.to_core()
-    backward(b1.g, 768, 256)
+    b1.g[...] = nn(ht[...], dcodes[:, 128:256])
     b1.to_core()
     for cp in a0.one + b0.one:
         left(cp)
@@ -437,7 +442,7 @@
             cp.wait_send()
 
 
-def pair_scratch(width):
+def pair_scratch(width, piece, over_z):
     chunk = [
         pltpu.VMEM((1024, width), F32),
         pltpu.VMEM((4, 2, 4, 16, width), BF16),
@@ -449,9 +454,10 @@
         pltpu.VMEM((3, 2, 16, width), BF16),
     ]
     shared = [
-        pltpu.VMEM((2, 4, 8, width), F32),
-        pltpu.VMEM((8, 8, width), F32),
-        pltpu.VMEM((4, 4, 8, width), F32),
+        pltpu.VMEM((2, 4, *piece), F32),
+        pltpu.VMEM((2, 4, *piece), over_z),
+        pltpu.VMEM((8, *piece), over_z),
+        pltpu.VMEM((4, 4, *piece), F32),
     ]
     return chunk + chunk + shared
 
@@ -459,13 +465,10 @@
 def assemble(whole0, whole1, out_first, out_second):
     for yy in range(NY):
         for ll in range(NL):
-            at = slice(yy * 16 + (ll // 2) * 8, yy * 16 + (ll // 2) * 8 + 8)
-            if ll % 2 == 0:
-                out_first[at, 384:768] = whole0[yy, ll]
-                out_second[at, :] = whole1[yy, ll]
-            else:
-                out_first[at, 0:384] = whole0[yy, ll]
-                out_first[at, 768:1024] = whole1[yy, ll]
+            first = (1 - ll // 2) * 512 + (ll % 2) * 256
+            out_first[yy * 16 : yy * 16 + 16, first : first + 256] = whole0[yy, ll]
+            at = yy * 16 + (ll // 2) * 8
+            out_second[at : at + 8, (ll % 2) * 128 : (ll % 2) * 128 + 128] = whole1[yy, ll]
 
 
 def shards(inputs, w_first, w_second, requests, slots, counts, edge_weight, offsets):
@@ -478,8 +481,8 @@
     whole0, whole1 = pl.pallas_call(
         lambda *refs: step(scale, *refs),
         out_shape=(
-            jax.ShapeDtypeStruct((NY, NL, 8, 384), F32),
-            jax.ShapeDtypeStruct((NY, NL, 8, 256), F32),
+            jax.ShapeDtypeStruct((NY, NL, 16, 256), F32),
+            jax.ShapeDtypeStruct((NY, NL, 8, 128), F32),
         ),
         in_specs=[anyplace] * 7 + [smem],
         out_specs=(vmem, vmem),
@@ -519,8 +522,8 @@
             pltpu.SemaphoreType.DMA((128,)),
             pltpu.SemaphoreType.DMA((128,)),
         ]
-        + pair_scratch(384)
-        + pair_scratch(256),
+        + pair_scratch(512, (16, 256), BF16)
+        + pair_scratch(128, (8, 128), F32),
         compiler_params=pltpu.CompilerParams(
             collective_id=0, has_side_effects=True, vmem_limit_bytes=56 << 20
         ),

time: 76.7 us -> 75.1 us (0.979)
  Pallas kernels: 75 us -> 73.8 us
    pallas_call x1, Pallas kernels: 73.2 us -> 72.1 us  [shards(): pl.pallas_call(lambda *refs: step(scale, *refs), out_shape=(jax.ShapeDtyp...]
where the time goes in v6:
time: 75.1 us; the launch traced here: 74.4 us
  Pallas kernels  73.8 us (98%)
    pallas_call x1, Pallas kernels, shards(): pl.pallas_call(lambda *refs: step(scale, *refs), out_shape=(jax.ShapeDtyp...  72.1 us
    pallas_call x1, Pallas kernels, shards(): pl.pallas_call(assemble, out_shape=(jax.ShapeDtypeStruct((64, 1024), F32)...  1.69 us

profile of v6, /device:TPU:32, one launch (start us, length us, event | category | flops | bytes accessed | tf_op | source)
XLA Modules:
  0.0 74.4 jit_solution(7381835759423124870)
XLA Ops:
  0.6 72.1 %embedding_step.1 = (f32[4,4,16,256]{3,2,1,0:T(8,128)}, f32[4,4,8,128]{3,2,1,0:T(8,128)}) custom-call(bf16[512,1024]{1,0:T(8,128)(2,1)} %refs_0_.1, bf16[1024,1024]{1,0:T(8,128)(2,1)} %refs_1_.1, bf16[1024,256]{1,0:T(8,128)(2,1)} %refs_2_.1, s32[16,128]{1,0:T(8,128)} %refs_3_.1, s32[15,512]{1,0:T(8,128)} %bitcast.3, s32[1,512]{1,0:T(1,128)} %bitcast.5, ...), custom_call_target="tpu_custom_call" | custom-call | flops 8999999488 | bytes 5000000 | tf_op jit(solution)/shard_map/embedding_step/pallas_call | solution.py:481
  72.7 1.7 %assemble.1 = (f32[64,1024]{1,0:T(8,128)}, f32[64,256]{1,0:T(8,128)}) custom-call(f32[4,4,16,256]{3,2,1,0:T(8,128)} %get-tuple-element.4.whole0, f32[4,4,8,128]{3,2,1,0:T(8,128)} %get-tuple-element.5.whole1), custom_call_target="tpu_custom_call" | custom-call | tf_op jit(solution)/shard_map/assemble/pallas_call | solution.py:535

commit v7 on v6

--- a/solution.py
+++ b/solution.py
@@ -117,7 +117,6 @@
             weights[part, pl.ds(r, 16), :] = total[part]
         return 0
 
-    lax.fori_loop(0, 8, weigh, 0)
 
     for cp in need_w1:
         cp.wait()
@@ -174,31 +173,32 @@
     lane = lax.broadcasted_iota(jnp.int32, (128, rows), 1).astype(F32)
     reply = {}
 
-    def deliver(block, b, j, e):
+    def deliver(block, b, e):
         cols = slice(0, 256) if e is None else slice(e * 128, e * 128 + 128)
-        got = nn(picks[b, j], block[:, cols]).astype(BF16)
-        dx, dc = j // 2, j % 2
-        spot = slice(b * 256 + dc * 128, b * 256 + dc * 128 + 128)
-        if j == 0:
-            table[0, spot, cols] = got
-        else:
-            found[b, j - 1, :, cols] = got
-            cp = copy(
-                found.at[b, j - 1, :, cols], table.at[dx, spot, cols],
-                device(xs(NX - dx), h, (c + dc) % 2, l, y),
-            )
-            cp.start()
-            reply.setdefault((b, dx), []).append(cp)
-
-    turns = (2, 6, 4, 3, 7, 5, 1, 0)
+        got = nn(picks[b].reshape(8 * 128, rows), block[:, cols]).astype(BF16)
+        found[b, :, :, cols] = got.reshape(8, 128, got.shape[1])
+        for j in turns:
+            dx, dc = j // 2, j % 2
+            spot = slice(b * 256 + dc * 128, b * 256 + dc * 128 + 128)
+            if j == 0:
+                table[0, spot, cols] = found[b, 0, :, cols]
+            else:
+                cp = copy(
+                    found.at[b, j, :, cols], table.at[dx, spot, cols],
+                    device(xs(NX - dx), h, (c + dc) % 2, l, y),
+                )
+                cp.start()
+                reply.setdefault((b, dx), []).append(cp)
+
+    turns = (4, 5, 2, 6, 3, 7, 1, 0)
+
     def choose(b):
         for j in turns:
             which = jnp.where((h + b) % 2 == 0, wishes[:, j * 8 : j * 8 + 1], wishes[:, j * 8 + 1 : j * 8 + 2])
             picks[b, j] = jnp.where(jnp.broadcast_to(which, (128, rows)) == lane, 1.0, 0.0).astype(BF16)
-            if b == 0:
-                deliver(sent, 0, j, None)
 
     choose(0)
+    deliver(sent, 0, None)
     for cp in to_next:
         left(cp)
     to_mate[1].start()
@@ -210,7 +210,7 @@
             recv_sem=recv_sem.at[11 + s - 1], device_id=device(x, h, c, l, ys(s)), device_id_type=MESH,
         )
         pl.when(y + s >= NY)(cp.start)
-    lax.fori_loop(8, rows // 16, weigh, 0)
+    lax.fori_loop(0, rows // 16, weigh, 0)
     choose(1)
     for g in range(8):
         ht[g * 128 : g * 128 + 128, :] = hidden[:, g * 128 : g * 128 + 128].T
@@ -267,8 +267,7 @@
 
     def serve_mate(e):
         to_mate[e].wait_recv()
-        for j in turns:
-            deliver(mate, 1, j, e)
+        deliver(mate, 1, e)
 
     attract(0)
     serve_mate(0)
@@ -416,8 +415,6 @@
     a1.to_core()
     b1.g[...] = nn(ht[...], dcodes[:, 128:256])
     b1.to_core()
-    for cp in a0.one + b0.one:
-        left(cp)
     a1.first()
     b1.first()
     b0.second()
@@ -505,7 +502,7 @@
             pltpu.VMEM((8, 8, 128), jnp.int32),
             pltpu.VMEM((8, 8, 128), jnp.int32),
             pltpu.VMEM((128, 512), F32),
-            pltpu.VMEM((2, 7, 128, 256), BF16),
+            pltpu.VMEM((2, 8, 128, 256), BF16),
             pltpu.VMEM((4, 512, 256), BF16),
             pltpu.VMEM((4, 512, 128), jnp.int32),
             pltpu.VMEM((512, 128), F32),

time: 75.1 us -> 73.9 us (0.984)
  Pallas kernels: 73.8 us -> 72.7 us
    pallas_call x1, Pallas kernels: 72.1 us -> 71 us  [shards(): pl.pallas_call(lambda *refs: step(scale, *refs), out_shape=(jax.ShapeDtyp...]
where the time goes in v7:
time: 73.9 us; the launch traced here: 73.3 us
  Pallas kernels  72.7 us (98%)
    pallas_call x1, Pallas kernels, shards(): pl.pallas_call(lambda *refs: step(scale, *refs), out_shape=(jax.ShapeDtyp...  71 us
    pallas_call x1, Pallas kernels, shards(): pl.pallas_call(assemble, out_shape=(jax.ShapeDtypeStruct((64, 1024), F32)...  1.69 us

profile of v7, /device:TPU:32, one launch (start us, length us, event | category | flops | bytes accessed | tf_op | source)
XLA Modules:
  0.0 73.3 jit_solution(9863935485625673177)
XLA Ops:
  0.6 71.0 %embedding_step.1 = (f32[4,4,16,256]{3,2,1,0:T(8,128)}, f32[4,4,8,128]{3,2,1,0:T(8,128)}) custom-call(bf16[512,1024]{1,0:T(8,128)(2,1)} %refs_0_.1, bf16[1024,1024]{1,0:T(8,128)(2,1)} %refs_1_.1, bf16[1024,256]{1,0:T(8,128)(2,1)} %refs_2_.1, s32[16,128]{1,0:T(8,128)} %refs_3_.1, s32[15,512]{1,0:T(8,128)} %bitcast.3, s32[1,512]{1,0:T(1,128)} %bitcast.5, ...), custom_call_target="tpu_custom_call" | custom-call | flops 8999999488 | bytes 5000000 | tf_op jit(solution)/shard_map/embedding_step/pallas_call | solution.py:478
  71.6 1.7 %assemble.1 = (f32[64,1024]{1,0:T(8,128)}, f32[64,256]{1,0:T(8,128)}) custom-call(f32[4,4,16,256]{3,2,1,0:T(8,128)} %get-tuple-element.4.whole0, f32[4,4,8,128]{3,2,1,0:T(8,128)} %get-tuple-element.5.whole1), custom_call_target="tpu_custom_call" | custom-call | tf_op jit(solution)/shard_map/assemble/pallas_call | solution.py:532

commit v8 on v7

--- a/solution.py
+++ b/solution.py
@@ -322,12 +322,14 @@
 
         def first(self):
             self.core.wait_recv()
-            for xx, hh, yy in each:
-                at = spot(self.kind, xx, hh, yy)
-                self.p_out[at] = (self.g[part_rows(xx, hh, c, yy), :] + self.c_in[at].astype(F32)).astype(BF16)
             self.one = []
             for s in (2, 1, 3):
                 at, target = self.near(s)
+                for hh in range(NH):
+                    for k in range(4):
+                        rows_at = part_rows(at, hh, c, k) if self.kind == "a" else part_rows(k, hh, c, at)
+                        both = self.g[rows_at, :] + self.c_in[at, hh, k].astype(F32)
+                        self.p_out[at, hh, k] = both.astype(BF16)
                 self.one.append(go(self.p_out.at[at], self.p_in.at[s - 1], target))
             mine = x if self.kind == "a" else y
             for far_at in range(4):

time: 73.9 us -> 73.6 us (level)
  no operation moved by 1% of the time
where the time goes in v8:
time: 73.6 us; the launch traced here: 73.2 us
  Pallas kernels  72.6 us (99%)
    pallas_call x1, Pallas kernels, shards(): pl.pallas_call(lambda *refs: step(scale, *refs), out_shape=(jax.ShapeDtyp...  70.9 us
    pallas_call x1, Pallas kernels, shards(): pl.pallas_call(assemble, out_shape=(jax.ShapeDtypeStruct((64, 1024), F32)...  1.69 us

profile of v8, /device:TPU:32, one launch (start us, length us, event | category | flops | bytes accessed | tf_op | source)
XLA Modules:
  0.0 73.2 jit_solution(6193149744688945386)
XLA Ops:
  0.6 70.9 %embedding_step.1 = (f32[4,4,16,256]{3,2,1,0:T(8,128)}, f32[4,4,8,128]{3,2,1,0:T(8,128)}) custom-call(bf16[512,1024]{1,0:T(8,128)(2,1)} %refs_0_.1, bf16[1024,1024]{1,0:T(8,128)(2,1)} %refs_1_.1, bf16[1024,256]{1,0:T(8,128)(2,1)} %refs_2_.1, s32[16,128]{1,0:T(8,128)} %refs_3_.1, s32[15,512]{1,0:T(8,128)} %bitcast.3, s32[1,512]{1,0:T(1,128)} %bitcast.5, ...), custom_call_target="tpu_custom_call" | custom-call | flops 8999999488 | bytes 5000000 | tf_op jit(solution)/shard_map/embedding_step/pallas_call | solution.py:480
  71.5 1.7 %assemble.1 = (f32[64,1024]{1,0:T(8,128)}, f32[64,256]{1,0:T(8,128)}) custom-call(f32[4,4,16,256]{3,2,1,0:T(8,128)} %get-tuple-element.4.whole0, f32[4,4,8,128]{3,2,1,0:T(8,128)} %get-tuple-element.5.whole1), custom_call_target="tpu_custom_call" | custom-call | tf_op jit(solution)/shard_map/assemble/pallas_call | solution.py:534
